TPU v7x, 32 devices: a whole 2x2x4 slice. The times are simulated.
32 devices in a mesh: group: 2 (over y), store: 4 (over x, core), head: 4 (over z).
Axes of the slice: x: 2, y: 2, z: 4, core: 2. Of those that a mesh axis runs over, the one named last changes fastest.
Arguments:
- saved: bfloat16 [192, 64, 5120], P(('group', 'store'), None, 'head'), parts along dimension 0, may hold values from -6 to 6
- fresh: bfloat16 [8, 256, 5120], P(('group', 'store')), parts along dimension 0, may hold values from -6 to 6
- w_query: bfloat16 [5120, 2048], P(None, 'head'), may hold values from -0.078125 to 0.078125
- w_key: bfloat16 [5120, 512], P(None, 'head'), may hold values from -0.078125 to 0.078125
- w_value: bfloat16 [5120, 512], P(None, 'head'), may hold values from -0.078125 to 0.078125
- q_gain: float32 [128], replicated, may hold values from 0.8 to 2
- k_gain: float32 [128], replicated, may hold values from 0.8 to 2
- lengths: int32 [8], P('group'), parts along dimension 0, may hold values from 1 to 64, 96 in all
- slot_page: int32 [192], P(('group', 'store')), parts along dimension 0, may hold values from 0 to 95, each once
Outputs:
- attended: bfloat16 [8, 256, 2048], P(('group', 'store'), None, 'head'), parts along dimension 0
There are 2 independent parts, one for each index of `group`. A program takes and returns all parts, laid end to end along the dimension named above; an argument that names none is the same for every part. Nothing has to cross between parts.
Inputs may be any that keep to these rules, and one draw needn't show every extreme that they name: The lengths of one group's sessions add up to 96, and the longest is exactly 64. Each value appears once in one group's slot_page.
All inputs are finite; a program needn't handle non-finite values.
Results may differ from a plain program's by a relative error of at most 0.0093.
Values may be sent and summed in bfloat16 or wider, within the bound.
A program may use at most 128 MiB of HBM per device.

v0:
```python
import math

import jax
import jax.numpy as jnp
from jax import lax
from jax.sharding import PartitionSpec as P

epsilon = 1e-06
rope_base = 1000000.0


def head_norm(values, gain):
    mean_sq = jnp.mean(values * values, axis=-1, keepdims=True)
    return values * lax.rsqrt(mean_sq + epsilon) * gain


def rotary(values, positions):
    width = values.shape[-1]
    half_width = width // 2
    expo = jnp.arange(half_width, dtype=jnp.float32) * (2.0 / width)
    freqs = jnp.exp(-expo * math.log(rope_base))
    angles = positions.astype(jnp.float32)[:, None] * freqs[None, :]
    cosine = jnp.cos(angles)[:, None, :]
    sine = jnp.sin(angles)[:, None, :]
    first = values[..., :half_width]
    second = values[..., half_width:]
    return jnp.concatenate(
        [first * cosine - second * sine, second * cosine + first * sine], axis=-1
    )


def shards(saved, fresh, w_query, w_key, w_value, q_gain, k_gain, lengths, slot_page):
    page_count, page_len, part_width = saved.shape
    head_dim = w_key.shape[1]
    w_pair = jnp.concatenate([w_key, w_value], axis=1)
    piece = lax.all_gather(saved, "head", axis=2, tiled=True)
    width = piece.shape[2]
    pair = jnp.dot(piece.reshape(-1, width), w_pair, preferred_element_type=jnp.float32)
    sess_count = lengths.shape[0]
    ends = jnp.cumsum(lengths)
    starts = ends - lengths
    session_of = jnp.sum((slot_page[:, None] >= ends[None, :]).astype(jnp.int32), axis=1)
    onehot = (session_of[:, None] == jnp.arange(sess_count, dtype=jnp.int32)[None, :]).astype(
        jnp.int32
    )
    first_page = jnp.sum(onehot * starts[None, :], axis=1)
    key_pos = ((slot_page - first_page) * page_len)[:, None] + jnp.arange(
        page_len, dtype=jnp.int32
    )[None, :]
    keys = rotary(head_norm(pair[:, None, :head_dim], k_gain), key_pos.reshape(-1)).astype(
        jnp.bfloat16
    )
    keys = keys.reshape(page_count, page_len, head_dim)
    values = pair[:, head_dim:].astype(jnp.bfloat16).reshape(page_count, page_len, head_dim)
    turn_rows = fresh[0]
    new_count = turn_rows.shape[0]
    group_heads = w_query.shape[1] // head_dim
    my_store = lax.axis_index("store")
    my_length = lax.dynamic_index_in_dim(lengths, my_store, 0, keepdims=False)
    new_pos = my_length * page_len + jnp.arange(new_count, dtype=jnp.int32)
    query_raw = jnp.dot(turn_rows, w_query, preferred_element_type=jnp.float32).reshape(
        new_count, group_heads, head_dim
    )
    queries = rotary(head_norm(query_raw, q_gain), new_pos).astype(jnp.bfloat16)
    new_raw = jnp.dot(turn_rows, w_key, preferred_element_type=jnp.float32)[:, None, :]
    new_keys = rotary(head_norm(new_raw, k_gain), new_pos).astype(jnp.bfloat16)[:, 0, :]
    new_values = jnp.dot(turn_rows, w_value, preferred_element_type=jnp.float32).astype(
        jnp.bfloat16
    )
    scale = math.sqrt(head_dim)
    every_query = lax.all_gather(queries[None], "store", axis=0, tiled=True)
    page_queries = jnp.take(every_query, session_of, axis=0)
    scores = (
        jnp.einsum("pqjd,pkd->pqjk", page_queries, keys, preferred_element_type=jnp.float32) / scale
    )
    weight = jnp.exp(scores)
    page_denom = jnp.sum(weight, axis=-1)
    page_numer = jnp.einsum(
        "pqjk,pkd->pqjd", weight.astype(jnp.bfloat16), values, preferred_element_type=jnp.float32
    )
    onehot_float = onehot.astype(jnp.float32)
    sess_numer = jnp.einsum(
        "ps,pqjd->sqjd", onehot_float, page_numer, precision=lax.Precision.HIGHEST
    )
    sess_denom = jnp.einsum(
        "ps,pqj->sqj", onehot_float, page_denom, precision=lax.Precision.HIGHEST
    )
    numer_all, denom_all = (
        lax.psum_scatter(sess_numer, "store", scatter_dimension=0, tiled=True),
        lax.psum_scatter(sess_denom, "store", scatter_dimension=0, tiled=True),
    )
    numer_in = numer_all[0]
    denom_in = denom_all[0]
    own_scores = (
        jnp.einsum("qjd,kd->qjk", queries, new_keys, preferred_element_type=jnp.float32) / scale
    )
    causal = jnp.arange(new_count)[None, :] <= jnp.arange(new_count)[:, None]
    own_weight = jnp.where(causal[:, None, :], jnp.exp(own_scores), jnp.float32(0.0))
    denom = denom_in + jnp.sum(own_weight, axis=-1)
    numer = numer_in + jnp.einsum(
        "qjk,kd->qjd",
        own_weight.astype(jnp.bfloat16),
        new_values,
        preferred_element_type=jnp.float32,
    )
    attended = (numer / denom[..., None]).astype(jnp.bfloat16)
    return attended.reshape(1, new_count, group_heads * head_dim)


def solution(mesh):
    return jax.shard_map(
        shards,
        mesh=mesh,
        in_specs=(
            P(("group", "store"), None, "head"),
            P(("group", "store"), None, None),
            P(None, "head"),
            P(None, "head"),
            P(None, "head"),
            P(),
            P(),
            P("group"),
            P(("group", "store")),
        ),
        out_specs=P(("group", "store"), None, "head"),
        check_vma=False,
    )
```

profile of v0, /device:TPU:0, one launch (start us, length us, event | category | flops | bytes accessed | tf_op | source)
XLA Modules:
  0.0 401.2 jit_solution(857535949752450444)
XLA Ops:
  6.6 8.0 %copy.66 = bf16[512,5120]{1,0:T(8,128)(2,1)} copy(bf16[512,5120]{0,1:T(8,128)(2,1)} %bitcast.86) | data formatting | bytes 10485760 | tf_op jit(solution)/shard_map/dot_general | solution.py:61
  14.6 4.1 %multiply_reduce_fusion.1 = (f32[256,4]{0,1:T(4,128)S(1)}, f32[256,4,128]{0,2,1:T(8,128)S(1)}) fusion(bf16[4,128,5120]{2,1,0:T(8,128)(2,1)} %bitcast.87, bf16[1,256,5120]{2,1,0:T(8,128)(2,1)S(1)} %copy-done), kind=kOutput, calls=%fused_computation.41 | convolution fusion | flops 1342438400 | bytes 8392704 | tf_op jit(solution)/shard_map/dot_general | solution.py:61
  20.8 0.8 copy.45
  23.8 17.5 %all-gather.3.cloned.1.call-done = bf16[4,256,4,128]{3,1,2,0:T(8,128)(2,1)} async-done(((bf16[1,256,4,128]{3,1,2,0:T(8,128)(2,1)}), bf16[4,256,4,128]{3,1,2,0:T(8,128)(2,1)}) %all-gather.3.cloned.1.call-update) | async-done | bytes 1048592 | tf_op jit(solution)/shard_map/all_gather | solution.py:71
  41.2 5.5 %gather_fusion = bf16[24,256,4,128]{3,1,2,0:T(8,128)(2,1)} fusion(bf16[4,256,4,128]{3,1,2,0:T(8,128)(2,1)} %all-gather.3.cloned.1.call-done, s32[1024]{0:T(1024)S(1)} %pad_clamp_fusion), kind=kCustom, calls=%fused_computation | custom fusion | bytes 12583008 | tf_op jit(solution)/shard_map/jit(_take)/gather | solution.py:72
  46.7 265.8 %all-gather.5.cloned.1.call-done = bf16[24,64,5120]{2,1,0:T(8,128)(2,1)} async-done(((bf16[24,64,1280]{2,1,0:T(8,128)(2,1)}), bf16[24,64,5120]{2,1,0:T(8,128)(2,1)}) %all-gather.5.cloned.1.call-update) | async-done | bytes 15728656 | tf_op jit(solution)/shard_map/all_gather | solution.py:36
  312.5 11.8 %convolution_bitcast_fusion = f32[1536,256]{0,1:T(8,128)} fusion(bf16[1536,5120]{1,0:T(8,128)(2,1)} %bitcast.94, bf16[5120,128]{1,0:T(8,128)(2,1)} %param.13, bf16[5120,128]{1,0:T(8,128)(2,1)} %param.12), kind=kOutput, calls=%fused_computation.12 | convolution fusion | flops 4031774720 | bytes 19922944 | tf_op jit(solution)/shard_map/dot_general | solution.py:38
  324.3 1.2 slice.66
  325.4 1.2 multiply_reduce_fusion
  326.9 1.3 multiply_bitcast_fusion
  328.1 2.3 fusion.38
  330.4 0.9 copy.68
  331.3 0.9 copy.67
  332.3 4.8 %fusion.5 = (f32[24,256,4]{1,2,0:T(4,128)S(1)}, f32[24,256,4,64]{1,3,2,0:T(8,128)S(1)}) fusion(bf16[24,64,64]{2,1,0:T(8,128)(2,1)} %bitcast.91, bf16[24,64,64]{2,1,0:T(8,128)(2,1)} %bitcast.92, bf16[24,256,4,128]{3,1,2,0:T(8,128)(2,1)} %gather_fusion, pred[24]{0:T(512)(128)(4,1)S(1)} %copy-done.14), kind=kOutput, calls=%fused_computation.7 | convolution fusion | flops 409706496 | bytes 13074456 | tf_op jit(solution)/shard_map/pqjd,pkd->pqjk/dot_general | solution.py:74
  337.1 2.0 fusion.7
  339.1 19.1 %fusion = f32[4,256,4,128]{3,0,2,1:T(4,128)S(1)} fusion(f32[24,256,4,128]{3,1,2,0:T(8,128)S(1)} %fusion.7, s32[24]{0:T(128)S(1)} %copy-done.9), kind=kOutput, calls=%fused_computation.1 | convolution fusion | flops 150995232 | bytes 14680160 | tf_op jit(solution)/shard_map/ps,pqjd->sqjd/dot_general | solution.py:82
  358.2 2.0 copy.50
  360.9 2.3 multiply_reduce_fusion.2
  363.7 1.2 fusion.75
  365.1 11.2 %all-reduce = f32[4,256,4]{1,2,0:T(4,128)S(1)} all-reduce(f32[4,256,4]{1,2,0:T(4,128)S(1)} %copy.57), channel_id=3, replica_groups=mesh['group'=2,'store'=4,'head'=4] {'store'}, use_global_device_ids=true, to_apply=%region_8.9.clone | all-reduce | flops 4096 | bytes 32768
  376.9 13.1 %reduce-scatter.2.cloned.1.call-done = f32[1,256,4,128]{3,1,2,0:T(8,128)} async-done(((f32[4,256,4,128]{3,1,2,0:T(8,128)}), f32[1,256,4,128]{3,1,2,0:T(8,128)}) %reduce-scatter.2.cloned.1.call-update) | async-done | bytes 524304 | tf_op jit(solution)/shard_map/reduce_scatter | solution.py:89
  390.0 1.2 copy.51
  391.3 2.6 fusion.23
  393.9 0.8 copy.58
  (64 shorter events, 5.6 us)
Async XLA Ops:
  6.5 8.1 %copy-start = (bf16[1,256,5120]{2,1,0:T(8,128)(2,1)S(1)}, bf16[1,256,5120]{2,1,0:T(8,128)(2,1)}, u32[]{:S(2)}) copy-start(bf16[1,256,5120]{2,1,0:T(8,128)(2,1)} %param.10) | copy-start | bytes 7864324
  6.5 34.7 %all-gather.3.cloned.1.call-start = ((), (), s32[]{:S(2)}) async-start(), calls=%async_computation.1 | async-start | bytes 1310720 | tf_op jit(solution)/shard_map/all_gather | solution.py:71
  6.6 13.4 %copy-start.3 = (f32[64]{0:T(128)}, f32[64]{0:T(128)S(1)}, u32[]{:S(2)}) copy-start(f32[64]{0:T(128)S(1)} %multiply_exponential_fusion.1) | copy-start | bytes 772
  14.6 4.1 %copy-start.11 = (s32[4]{0:T(128)S(1)}, s32[4]{0:T(128)}, u32[]{:S(2)}) copy-start(s32[4]{0:T(128)} %param.16) | copy-start | bytes 52
  14.6 6.0 %copy-start.10 = (f32[128]{0:T(128)S(1)}, f32[128]{0:T(128)}, u32[]{:S(2)}) copy-start(f32[128]{0:T(128)} %param.14) | copy-start | bytes 1540
  18.7 4.1 %copy-start.12 = (s32[24]{0:T(128)S(1)}, s32[24]{0:T(128)}, u32[]{:S(2)}) copy-start(s32[24]{0:T(128)} %param.17) | copy-start | bytes 292
  20.0 0.6 copy-start.5
  20.8 25.9 %copy-start.1 = (bf16[256,4,64]{0,2,1:T(8,128)(2,1)}, bf16[256,4,64]{0,2,1:T(8,128)(2,1)S(1)}, u32[]{:S(2)}) copy-start(bf16[256,4,64]{0,2,1:T(8,128)(2,1)S(1)} %get-tuple-element.8) | copy-start | bytes 393220
  21.7 290.8 %all-gather.5.cloned.1.call-start = ((), (), s32[]{:S(2)}) async-start(), calls=%async_computation.2 | async-start | bytes 19660800 | tf_op jit(solution)/shard_map/all_gather | solution.py:36
  22.4 367.6 %reduce-scatter.2.cloned.1.call-start = ((), (), s32[]{:S(2)}) async-start(), calls=%async_computation.3 | async-start | bytes 2621440 | tf_op jit(solution)/shard_map/reduce_scatter | solution.py:89
  22.9 23.8 %copy-start.8 = (s32[24]{0:T(128)}, s32[24]{0:T(128)S(1)}, u32[]{:S(2)}) copy-start(s32[24]{0:T(128)S(1)} %convert_reduce_fusion) | copy-start | bytes 292
  326.9 5.4 %copy-start.14 = (pred[24]{0:T(512)(128)(4,1)S(1)}, pred[24]{0:T(512)(128)(4,1)}, u32[]{:S(2)}) copy-start(pred[24]{0:T(512)(128)(4,1)} %compare_and_fusion) | copy-start | bytes 76
  337.1 2.0 copy-start.9
  358.2 2.0 copy-start.13
  360.2 3.0 copy-start.7
  360.2 3.1 copy-start.4
  360.2 3.1 copy-start.6
  360.2 3.4 copy-start.2
Sparse Core Ops, SparseCore 0:
  21.8 19.4 all-gather.2
  42.8 269.6 all-gather.4
  360.4 29.6 reduce-scatter.1
where the time goes:
time: 402 us; the launch traced here: 401 us
  waiting for transfers between devices  297 us (74%)
  matrix products  48 us (12%)
  local copies, waits for them, and re-layouts  23.2 us (6%)
  between operations  14.1 us (4%)
  blocking collectives  11.2 us (3%)
  other arithmetic  7.38 us (2%)
    all_gather x1, waiting for transfers between devices, shards(): piece = lax.all_gather(saved, 'head', axis=2, tiled=True)  266 us
    dot_general x1, matrix products, shards(): jnp.einsum('ps,pqjd->sqjd', onehot_float, page_numer, precision=lax.Preci...  19.1 us
    all_gather x1, waiting for transfers between devices, shards(): every_query = lax.all_gather(queries[None], 'store', axis=0, tiled=True)  17.5 us
    reduce_scatter x1, waiting for transfers between devices, shards(): lax.psum_scatter(sess_numer, 'store', scatter_dimension=0, tiled=True)  13.1 us
    dot_general x1, matrix products, shards(): jnp.dot(piece.reshape(-1, width), w_pair, preferred_element_type=jnp.floa...  11.8 us
    unnamed x1, blocking collectives  11.2 us
  transfers between devices with their start and end apart: 3, of which 3 were waited for; matrix products, arithmetic and copies ran while one was open for 3% of the time, Pallas kernels for 0%

commit v1 on v0

--- a/solution.py
+++ b/solution.py
@@ -33,9 +33,16 @@
     page_count, page_len, part_width = saved.shape
     head_dim = w_key.shape[1]
     w_pair = jnp.concatenate([w_key, w_value], axis=1)
-    piece = lax.all_gather(saved, "head", axis=2, tiled=True)
-    width = piece.shape[2]
-    pair = jnp.dot(piece.reshape(-1, width), w_pair, preferred_element_type=jnp.float32)
+    n_head = lax.axis_size("head")
+    w_here = lax.all_to_all(
+        w_pair.reshape(n_head, part_width, 2 * head_dim), "head", 0, 0, tiled=True
+    )
+    rows = saved.reshape(-1, part_width)
+    partial = jnp.einsum(
+        "rf,hfc->hrc", rows, w_here, preferred_element_type=jnp.float32
+    ).astype(jnp.bfloat16)
+    parts = lax.all_to_all(partial, "head", 0, 0, tiled=True)
+    pair = jnp.sum(parts.astype(jnp.float32), axis=0)
     sess_count = lengths.shape[0]
     ends = jnp.cumsum(lengths)
     starts = ends - lengths

time: 402 us -> 241 us (0.60)
  waiting for transfers between devices: 297 us -> 63.3 us
  blocking collectives: 11.2 us -> 76.1 us
  matrix products: 48 us -> 41.9 us
  other arithmetic: 7.38 us -> 12.5 us
  starting transfers between devices: 0.26 us -> 4.73 us
  local copies, waits for them, and re-layouts: 23.2 us -> 27.5 us
    all_gather x1 -> x0, waiting for transfers between devices: 266 us -> none  [shards(): piece = lax.all_gather(saved, 'head', axis=2, tiled=True)]
    all_to_all x0 -> x1, blocking collectives: none -> 66 us  [shards(): lax.all_to_all(w_pair.reshape(n_head, part_width, 2 * head_dim), 'head',...]
    all_to_all x0 -> x1, waiting for transfers between devices: none -> 31.1 us  [shards(): parts = lax.all_to_all(partial, 'head', 0, 0, tiled=True)]
    dot_general x1, matrix products: 11.8 us -> 5.7 us  [shards(): jnp.einsum('rf,hfc->hrc', rows, w_here, preferred_element_type=jnp.float32)]
    all_to_all x0 -> x1, starting transfers between devices: none -> 4.64 us  [shards(): parts = lax.all_to_all(partial, 'head', 0, 0, tiled=True)]
    reshape x0 -> x1, local copies, waits for them, and re-layouts: none -> 4.39 us  [shards(): w_pair.reshape(n_head, part_width, 2 * head_dim)]
  transfers between devices with their start and end apart: 3 -> 3, of which waited for: 3 -> 3; matrix products, arithmetic and copies ran while one was open for 3% -> 11% of each run, Pallas kernels for 0% -> 0%
where the time goes in v1:
time: 241 us; the launch traced here: 240 us
  blocking collectives  76.1 us (32%)
  waiting for transfers between devices  63.3 us (26%)
  matrix products  41.9 us (17%)
  local copies, waits for them, and re-layouts  27.5 us (11%)
  between operations  14.4 us (6%)
  other arithmetic  12.5 us (5%)
  starting transfers between devices  4.73 us (2%)
    all_to_all x1, blocking collectives, shards(): lax.all_to_all(w_pair.reshape(n_head, part_width, 2 * head_dim), 'head',...  66 us
    all_to_all x1, waiting for transfers between devices, shards(): parts = lax.all_to_all(partial, 'head', 0, 0, tiled=True)  31.1 us
    dot_general x1, matrix products, shards(): jnp.einsum('ps,pqjd->sqjd', onehot_float, page_numer, precision=lax.Preci...  19.1 us
    all_gather x1, waiting for transfers between devices, shards(): every_query = lax.all_gather(queries[None], 'store', axis=0, tiled=True)  17.1 us
    reduce_scatter x1, waiting for transfers between devices, shards(): lax.psum_scatter(sess_numer, 'store', scatter_dimension=0, tiled=True)  15 us
    unnamed x1, blocking collectives  10.1 us
    dot_general x1, local copies, waits for them, and re-layouts, shards(): jnp.dot(turn_rows, w_query, preferred_element_type=jnp.float32)  8.08 us
    dot_general x1, matrix products, shards(): jnp.einsum('rf,hfc->hrc', rows, w_here, preferred_element_type=jnp.float32)  5.7 us
  transfers between devices with their start and end apart: 3, of which 3 were waited for; matrix products, arithmetic and copies ran while one was open for 11% of the time, Pallas kernels for 0%

profile of v1, /device:TPU:0, one launch (start us, length us, event | category | flops | bytes accessed | tf_op | source)
XLA Modules:
  0.0 240.4 jit_solution(951474106398837915)
XLA Ops:
  6.5 3.7 %pad_maximum_fusion = bf16[5120,256]{1,0:T(8,128)(2,1)} fusion(bf16[5120,128]{1,0:T(8,128)(2,1)} %param.13, bf16[5120,128]{1,0:T(8,128)(2,1)} %param.12), kind=kLoop, calls=%fused_computation.15 | loop fusion | flops 5242880 | bytes 5242880 | tf_op jit(solution)/shard_map/concatenate | solution.py:35
  10.2 4.4 %copy.43 = bf16[4,1280,256]{1,2,0:T(8,128)(2,1)} copy(bf16[4,1280,256]{2,1,0:T(8,128)(2,1)} %bitcast.90) | data formatting | bytes 5242880 | tf_op jit(solution)/shard_map/reshape | solution.py:38
  14.6 66.0 %all_to_all.10 = bf16[4,1280,256]{1,2,0:T(8,128)(2,1)S(1)} all-to-all(bf16[4,1280,256]{1,2,0:T(8,128)(2,1)} %copy.43), channel_id=1, replica_groups=mesh['group'=2,'store'=4,'head'=4] {'head'}, dimensions={0} | all-to-all | bytes 5242880 | tf_op jit(solution)/shard_map/all_to_all | solution.py:37
  80.6 5.7 %fusion.7 = bf16[4,1536,256]{1,2,0:T(8,128)(2,1)} fusion(bf16[4,1280,256]{1,2,0:T(8,128)(2,1)S(1)} %all_to_all.10, bf16[1536,1280,1]{1,0,2:T(8,128)(2,1)S(1)} %bitcast.99), kind=kOutput, calls=%fused_computation.11 | convolution fusion | flops 4028104704 | bytes 9699328 | tf_op jit(solution)/shard_map/rf,hfc->hrc/dot_general | solution.py:41
  86.3 4.6 %all-to-all-start.1 = ((bf16[4,1536,256]{1,2,0:T(8,128)(2,1)}), bf16[4,1536,256]{1,2,0:T(8,128)(2,1)}, u32[]{:S(2)}, u32[]{:S(2)}) async-start(bf16[4,1536,256]{1,2,0:T(8,128)(2,1)} %fusion.7), calls=%async_computation.1 | async-start | bytes 6291456 | tf_op jit(solution)/shard_map/all_to_all | solution.py:44
  91.0 8.1 %copy.64 = bf16[512,5120]{1,0:T(8,128)(2,1)} copy(bf16[512,5120]{0,1:T(8,128)(2,1)} %bitcast.91) | data formatting | bytes 10485760 | tf_op jit(solution)/shard_map/dot_general | solution.py:68
  100.4 4.1 %multiply_reduce_fusion.1 = (f32[256,4]{0,1:T(4,128)S(1)}, f32[256,4,128]{0,2,1:T(8,128)S(1)}) fusion(bf16[4,128,5120]{2,1,0:T(8,128)(2,1)} %bitcast.92, bf16[1,256,5120]{2,1,0:T(8,128)(2,1)S(1)} %copy-done), kind=kOutput, calls=%fused_computation.41 | convolution fusion | flops 1342438400 | bytes 8392704 | tf_op jit(solution)/shard_map/dot_general | solution.py:68
  107.0 17.1 %all-gather.2.cloned.1.call-done = bf16[4,256,4,128]{3,1,2,0:T(8,128)(2,1)} async-done(((bf16[1,256,4,128]{3,1,2,0:T(8,128)(2,1)}), bf16[4,256,4,128]{3,1,2,0:T(8,128)(2,1)}) %all-gather.2.cloned.1.call-update) | async-done | bytes 1048592 | tf_op jit(solution)/shard_map/all_gather | solution.py:78
  124.2 5.5 %gather_fusion = bf16[24,256,4,128]{3,1,2,0:T(8,128)(2,1)} fusion(bf16[4,256,4,128]{3,1,2,0:T(8,128)(2,1)} %all-gather.2.cloned.1.call-done, s32[1024]{0:T(1024)S(1)} %pad_clamp_fusion), kind=kCustom, calls=%fused_computation | custom fusion | bytes 12583008 | tf_op jit(solution)/shard_map/jit(_take)/gather | solution.py:79
  129.7 31.1 %all-to-all-done.1 = bf16[4,1536,256]{1,2,0:T(8,128)(2,1)} async-done(((bf16[4,1536,256]{1,2,0:T(8,128)(2,1)}), bf16[4,1536,256]{1,2,0:T(8,128)(2,1)}, u32[]{:S(2)}, u32[]{:S(2)}) %all-to-all-start.1) | async-done | bytes 3145760 | tf_op jit(solution)/shard_map/all_to_all | solution.py:44
  160.8 2.6 %convert_reduce_fusion = f32[1536,256]{0,1:T(8,128)S(1)} fusion(bf16[4,1536,256]{1,2,0:T(8,128)(2,1)} %all-to-all-done.1), kind=kLoop, calls=%fused_computation.4 | loop fusion | flops 2752512 | bytes 4718592 | tf_op jit(solution)/shard_map/reduce_sum | solution.py:45
  163.5 1.1 copy-done.1
  164.9 1.3 multiply_bitcast_fusion
  166.1 2.3 fusion.36
  170.4 4.8 %fusion.5 = (f32[24,256,4]{1,2,0:T(4,128)S(1)}, f32[24,256,4,64]{1,3,2,0:T(8,128)S(1)}) fusion(bf16[24,64,64]{2,1,0:T(8,128)(2,1)} %bitcast.96, bf16[24,64,64]{2,1,0:T(8,128)(2,1)} %bitcast.97, bf16[24,256,4,128]{3,1,2,0:T(8,128)(2,1)} %gather_fusion, pred[24]{0:T(512)(128)(4,1)S(1)} %copy-done.16), kind=kOutput, calls=%fused_computation.8 | convolution fusion | flops 409706496 | bytes 13074456 | tf_op jit(solution)/shard_map/pqjd,pkd->pqjk/dot_general | solution.py:81
  175.2 2.0 fusion.8
  177.2 19.1 %fusion = f32[4,256,4,128]{3,0,2,1:T(4,128)S(1)} fusion(f32[24,256,4,128]{3,1,2,0:T(8,128)S(1)} %fusion.8, s32[24]{0:T(128)S(1)} %copy-done.10), kind=kOutput, calls=%fused_computation.1 | convolution fusion | flops 150995232 | bytes 14680160 | tf_op jit(solution)/shard_map/ps,pqjd->sqjd/dot_general | solution.py:89
  196.2 2.0 copy.48
  198.9 2.3 multiply_reduce_fusion.2
  201.7 1.2 fusion.72
  203.1 10.1 %all-reduce = f32[4,256,4]{1,2,0:T(4,128)S(1)} all-reduce(f32[4,256,4]{1,2,0:T(4,128)S(1)} %copy.55), channel_id=3, replica_groups=mesh['group'=2,'store'=4,'head'=4] {'store'}, use_global_device_ids=true, to_apply=%region_9.10.clone | all-reduce | flops 4096 | bytes 32768
  213.9 15.0 %reduce-scatter.2.cloned.1.call-done = f32[1,256,4,128]{3,1,2,0:T(8,128)} async-done(((f32[4,256,4,128]{3,1,2,0:T(8,128)}), f32[1,256,4,128]{3,1,2,0:T(8,128)}) %reduce-scatter.2.cloned.1.call-update) | async-done | bytes 524304 | tf_op jit(solution)/shard_map/reduce_scatter | solution.py:96
  228.9 1.2 copy.49
  230.2 2.6 %fusion.21 = bf16[256,4,128]{0,2,1:T(8,128)(2,1)S(1)} fusion(bf16[5120,128]{1,0:T(8,128)(2,1)} %param.13, bf16[1,256,5120]{2,1,0:T(8,128)(2,1)S(1)} %copy-done, f32[1,256,4,128]{1,3,2,0:T(8,128)S(1)} %copy.49, bf16[256,4,256]{0,2,1:T(8,128)(2,1)} %get-tuple-element.18, f32[256,4]{0,1:T(4,128)S(1)} %fusion.58), kind=kOutput, calls=%fused_computation.27 | convolution fusion | flops 403079168 | bytes 5246976 | tf_op jit(solution)/shard_map/qjk,kd->qjd/dot_general | solution.py:107
  (71 shorter events, 8.1 us)
Async XLA Ops:
  6.5 93.9 %copy-start = (bf16[1,256,5120]{2,1,0:T(8,128)(2,1)S(1)}, bf16[1,256,5120]{2,1,0:T(8,128)(2,1)}, u32[]{:S(2)}) copy-start(bf16[1,256,5120]{2,1,0:T(8,128)(2,1)} %param.10) | copy-start | bytes 7864324
  14.6 66.0 %copy-start.12 = (bf16[24,64,1280]{2,1,0:T(8,128)(2,1)S(1)}, bf16[24,64,1280]{2,1,0:T(8,128)(2,1)}, u32[]{:S(2)}) copy-start(bf16[24,64,1280]{2,1,0:T(8,128)(2,1)} %param.9) | copy-start | bytes 11796484
  86.3 74.5 %all-to-all-start.1 = ((bf16[4,1536,256]{1,2,0:T(8,128)(2,1)}), bf16[4,1536,256]{1,2,0:T(8,128)(2,1)}, u32[]{:S(2)}, u32[]{:S(2)}) async-start(bf16[4,1536,256]{1,2,0:T(8,128)(2,1)} %fusion.7), calls=%async_computation.1 | async-start | bytes 6291456 | tf_op jit(solution)/shard_map/all_to_all | solution.py:44
  91.0 33.2 %all-gather.2.cloned.1.call-start = ((), (), s32[]{:S(2)}) async-start(), calls=%async_computation.3 | async-start | bytes 1310720 | tf_op jit(solution)/shard_map/all_gather | solution.py:78
  91.0 8.1 %copy-start.13 = (s32[4]{0:T(128)S(1)}, s32[4]{0:T(128)}, u32[]{:S(2)}) copy-start(s32[4]{0:T(128)} %param.16) | copy-start | bytes 52
  100.4 4.1 %copy-start.4 = (f32[64]{0:T(128)}, f32[64]{0:T(128)S(1)}, u32[]{:S(2)}) copy-start(f32[64]{0:T(128)S(1)} %multiply_exponential_fusion.1) | copy-start | bytes 772
  100.4 4.1 %copy-start.6 = (f32[256]{0:T(256)}, f32[256]{0:T(256)S(1)}, u32[]{:S(2)}) copy-start(f32[256]{0:T(256)S(1)} %add_convert_fusion.2) | copy-start | bytes 3076
  100.4 4.4 %copy-start.11 = (f32[128]{0:T(128)S(1)}, f32[128]{0:T(128)}, u32[]{:S(2)}) copy-start(f32[128]{0:T(128)} %param.14) | copy-start | bytes 1540
  104.5 1.7 copy-start.14
  105.0 24.7 %copy-start.2 = (bf16[256,4,64]{0,2,1:T(8,128)(2,1)}, bf16[256,4,64]{0,2,1:T(8,128)(2,1)S(1)}, u32[]{:S(2)}) copy-start(bf16[256,4,64]{0,2,1:T(8,128)(2,1)S(1)} %get-tuple-element.8) | copy-start | bytes 393220
  105.9 123.0 %reduce-scatter.2.cloned.1.call-start = ((), (), s32[]{:S(2)}) async-start(), calls=%async_computation.4 | async-start | bytes 2621440 | tf_op jit(solution)/shard_map/reduce_scatter | solution.py:96
  106.3 23.5 %copy-start.9 = (s32[24]{0:T(128)}, s32[24]{0:T(128)S(1)}, u32[]{:S(2)}) copy-start(s32[24]{0:T(128)S(1)} %convert_reduce_fusion.1) | copy-start | bytes 292
  163.4 1.1 copy-start.1
  164.9 5.5 %copy-start.16 = (pred[24]{0:T(512)(128)(4,1)S(1)}, pred[24]{0:T(512)(128)(4,1)}, u32[]{:S(2)}) copy-start(pred[24]{0:T(512)(128)(4,1)} %compare_and_fusion) | copy-start | bytes 76
  175.2 2.0 copy-start.10
  196.2 2.0 copy-start.15
  198.2 3.0 %copy-start.8 = (f32[128]{0:T(128)S(1)}, f32[128]{0:T(128)}, u32[]{:S(2)}) copy-start(f32[128]{0:T(128)} %param.15) | copy-start | bytes 1540
  198.2 3.1 %copy-start.5 = (f32[64]{0:T(128)S(1)}, f32[64]{0:T(128)}, u32[]{:S(2)}) copy-start(f32[64]{0:T(128)} %copy-done.4) | copy-start | bytes 772
  198.2 3.1 %copy-start.7 = (f32[256]{0:T(256)S(1)}, f32[256]{0:T(256)}, u32[]{:S(2)}) copy-start(f32[256]{0:T(256)} %copy-done.6) | copy-start | bytes 3076
  198.2 3.5 %copy-start.3 = (bf16[256,4,64]{0,2,1:T(8,128)(2,1)S(1)}, bf16[256,4,64]{0,2,1:T(8,128)(2,1)}, u32[]{:S(2)}) copy-start(bf16[256,4,64]{0,2,1:T(8,128)(2,1)} %copy-done.2) | copy-start | bytes 393220
Sparse Core Ops, SparseCore 0:
  106.1 18.0 all-gather.1
  198.4 30.4 reduce-scatter.1

commit v2 on v0

v2 whole, which is shorter than its diff:
```python
import functools
import math

import jax
import jax.numpy as jnp
from jax import lax
from jax.experimental import pallas as pl
from jax.experimental.pallas import tpu as pltpu
from jax.sharding import PartitionSpec as P

epsilon = 1e-06
rope_base = 1000000.0
part_scale = 16.0


def head_norm(values, gain):
    mean_sq = jnp.mean(values * values, axis=-1, keepdims=True)
    return values * lax.rsqrt(mean_sq + epsilon) * gain


def rotary(values, positions):
    width = values.shape[-1]
    half_width = width // 2
    expo = jnp.arange(half_width, dtype=jnp.float32) * (2.0 / width)
    freqs = jnp.exp(-expo * math.log(rope_base))
    angles = positions.astype(jnp.float32)[:, None] * freqs[None, :]
    cosine = jnp.cos(angles)[:, None, :]
    sine = jnp.sin(angles)[:, None, :]
    first = values[..., :half_width]
    second = values[..., half_width:]
    return jnp.concatenate(
        [first * cosine - second * sine, second * cosine + first * sine], axis=-1
    )


def page_kernel(scale, session_ref, q_ref, k_ref, v_ref, numer_ref, denom_ref, numer, denom):
    pages = k_ref.shape[0]
    page_len = k_ref.shape[1]
    numer[...] = jnp.zeros_like(numer)
    denom[...] = jnp.zeros_like(denom)

    def body(p, carry):
        s = session_ref[p]
        scores = jnp.dot(k_ref[p], q_ref[s], preferred_element_type=jnp.float32)
        weight = jnp.exp(scores * scale)
        denom[s] += jnp.sum(weight.reshape(page_len // 8, 8, weight.shape[-1]), axis=0)
        numer[s] += lax.dot_general(
            v_ref[p],
            weight.astype(jnp.bfloat16),
            (((0,), (0,)), ((), ())),
            preferred_element_type=jnp.float32,
        )
        return carry

    lax.fori_loop(0, pages, body, 0, unroll=2)
    numer_ref[...] = numer[...].astype(jnp.bfloat16)
    denom_ref[...] = denom[...]


def page_attention(session_of, queries, keys, values, scale):
    sess_count, head_dim, columns = queries.shape
    return pl.pallas_call(
        functools.partial(page_kernel, scale),
        out_shape=(
            jax.ShapeDtypeStruct((sess_count, head_dim, columns), jnp.bfloat16),
            jax.ShapeDtypeStruct((sess_count, 8, columns), jnp.float32),
        ),
        in_specs=[pl.BlockSpec(memory_space=pltpu.SMEM)]
        + [pl.BlockSpec(memory_space=pltpu.VMEM)] * 3,
        out_specs=[pl.BlockSpec(memory_space=pltpu.VMEM)] * 2,
        scratch_shapes=[
            pltpu.VMEM((sess_count, head_dim, columns), jnp.float32),
            pltpu.VMEM((sess_count, 8, columns), jnp.float32),
        ],
        compiler_params=pltpu.CompilerParams(vmem_limit_bytes=48 * 1024 * 1024),
        cost_estimate=pl.CostEstimate(
            flops=4 * keys.size * columns, bytes_accessed=6 << 20, transcendentals=0
        ),
    )(session_of, queries, keys, values)


def shards(saved, fresh, w_query, w_key, w_value, q_gain, k_gain, lengths, slot_page):
    page_count, page_len, part_width = saved.shape
    head_dim = w_key.shape[1]
    n_head = lax.axis_size("head")
    n_store = lax.axis_size("store")
    my_store = lax.axis_index("store")
    sess_count = lengths.shape[0]
    share = part_width // n_store

    def my_rows(w):
        cut = w.reshape(n_head, n_store, share, head_dim)
        return lax.dynamic_index_in_dim(cut, my_store, 1, keepdims=False)

    w_share = jnp.concatenate([my_rows(w_key), my_rows(w_value)], axis=2)
    w_share = lax.all_to_all(w_share, "head", 0, 0, tiled=True)
    w_here = lax.all_gather(w_share, "store", axis=1, tiled=True)
    rows = saved.reshape(-1, part_width)
    partial = (
        jnp.einsum("rf,hfc->hrc", rows, w_here, preferred_element_type=jnp.float32) * part_scale
    ).astype(jnp.float16)
    parts = lax.all_to_all(partial, "head", 0, 0, tiled=True)
    pair = jnp.sum(parts.astype(jnp.float32), axis=0) * (1.0 / part_scale)

    ends = jnp.cumsum(lengths)
    starts = ends - lengths
    session_of = jnp.sum((slot_page[:, None] >= ends[None, :]).astype(jnp.int32), axis=1)
    onehot = (session_of[:, None] == jnp.arange(sess_count, dtype=jnp.int32)[None, :]).astype(
        jnp.int32
    )
    first_page = jnp.sum(onehot * starts[None, :], axis=1)
    key_pos = ((slot_page - first_page) * page_len)[:, None] + jnp.arange(
        page_len, dtype=jnp.int32
    )[None, :]
    keys = rotary(head_norm(pair[:, None, :head_dim], k_gain), key_pos.reshape(-1)).astype(
        jnp.bfloat16
    )
    keys = keys.reshape(page_count, page_len, head_dim)
    values = pair[:, head_dim:].astype(jnp.bfloat16).reshape(page_count, page_len, head_dim)

    turn_rows = fresh[0]
    new_count = turn_rows.shape[0]
    group_heads = w_query.shape[1] // head_dim
    my_length = lax.dynamic_index_in_dim(lengths, my_store, 0, keepdims=False)
    new_pos = my_length * page_len + jnp.arange(new_count, dtype=jnp.int32)
    query_raw = jnp.dot(turn_rows, w_query, preferred_element_type=jnp.float32).reshape(
        new_count, group_heads, head_dim
    )
    queries = rotary(head_norm(query_raw, q_gain), new_pos).astype(jnp.bfloat16)
    new_raw = jnp.dot(turn_rows, w_key, preferred_element_type=jnp.float32)[:, None, :]
    new_keys = rotary(head_norm(new_raw, k_gain), new_pos).astype(jnp.bfloat16)[:, 0, :]
    new_values = jnp.dot(turn_rows, w_value, preferred_element_type=jnp.float32).astype(
        jnp.bfloat16
    )
    scale = 1.0 / math.sqrt(head_dim)
    columns = group_heads * new_count
    q_t = queries.transpose(2, 1, 0).reshape(head_dim, columns)
    every_query = lax.all_gather(q_t, "store", axis=0)

    numer_t, denom_8 = page_attention(session_of, every_query, keys, values, scale)
    denom = jnp.sum(denom_8, axis=1)
    high = denom.astype(jnp.bfloat16)
    low = (denom - high.astype(jnp.float32)).astype(jnp.bfloat16)
    sent = jnp.concatenate([numer_t, high[:, None, :], low[:, None, :]], axis=1)
    got = lax.all_to_all(sent, "store", 0, 0, tiled=True)
    total = jnp.sum(got.astype(jnp.float32), axis=0)

    own_scores = jnp.dot(new_keys, q_t, preferred_element_type=jnp.float32) * scale
    token = jnp.arange(columns, dtype=jnp.int32) % new_count
    causal = jnp.arange(new_count)[:, None] <= token[None, :]
    own_weight = jnp.where(causal, jnp.exp(own_scores), jnp.float32(0.0))
    own_denom = jnp.sum(own_weight, axis=0)
    own_numer = jnp.einsum(
        "kd,kc->dc", new_values, own_weight.astype(jnp.bfloat16), preferred_element_type=jnp.float32
    )
    numer = total[:head_dim] + own_numer
    denom = total[head_dim] + total[head_dim + 1] + own_denom
    attended = (numer / denom[None, :]).astype(jnp.bfloat16)
    attended = attended.reshape(head_dim, group_heads, new_count).transpose(2, 1, 0)
    return attended.reshape(1, new_count, group_heads * head_dim)


def solution(mesh):
    return jax.shard_map(
        shards,
        mesh=mesh,
        in_specs=(
            P(("group", "store"), None, "head"),
            P(("group", "store"), None, None),
            P(None, "head"),
            P(None, "head"),
            P(None, "head"),
            P(),
            P(),
            P("group"),
            P(("group", "store")),
        ),
        out_specs=P(("group", "store"), None, "head"),
        check_vma=False,
    )
```

time: 402 us -> 198 us (0.49)
  waiting for transfers between devices: 297 us -> 91.1 us
  matrix products: 48 us -> 19.6 us
  blocking collectives: 11.2 us -> 23.5 us
  starting transfers between devices: 0.26 us -> 9.31 us
  Pallas kernels: 0 us -> 8.07 us
  other arithmetic: 7.38 us -> 13.6 us
  local copies, waits for them, and re-layouts: 23.2 us -> 17.7 us
    all_gather x2, waiting for transfers between devices: 283 us -> 24.8 us  [the longest x1 24.8 us: shards(): w_here = lax.all_gather(w_share, 'store', axis=1, tiled=True)]
    all_to_all x0 -> x2, waiting for transfers between devices: none -> 66.2 us  [the longest x1 52.9 us: shards(): parts = lax.all_to_all(partial, 'head', 0, 0, tiled=True)]
    dot_general x7 -> x3, matrix products: 41.6 us -> 12.6 us  [the longest x1 8.84 us: shards(): jnp.einsum('rf,hfc->hrc', rows, w_here, preferred_element_type=jnp.float32)]
    all_to_all x0 -> x1, blocking collectives: none -> 23.5 us  [shards(): w_share = lax.all_to_all(w_share, 'head', 0, 0, tiled=True)]
    reduce_scatter x1 -> x0, waiting for transfers between devices: 13.1 us -> none  [shards(): lax.psum_scatter(sess_numer, 'store', scatter_dimension=0, tiled=True)]
    unnamed x1 -> x0, blocking collectives: 11.2 us -> none
    all_to_all x0 -> x2, starting transfers between devices: none -> 9.26 us  [the longest x1 4.82 us: shards(): parts = lax.all_to_all(partial, 'head', 0, 0, tiled=True)]
    pallas_call x0 -> x1, Pallas kernels: none -> 8.07 us  [page_attention(): pl.pallas_call(functools.partial(page_kernel, scale), out_shape=(jax.Shap...]
  transfers between devices with their start and end apart: 3 -> 4, of which waited for: 3 -> 3; matrix products, arithmetic and copies ran while one was open for 3% -> 15% of each run, Pallas kernels for 0% -> 0%
where the time goes in v2:
time: 198 us; the launch traced here: 197 us
  waiting for transfers between devices  91.1 us (46%)
  blocking collectives  23.5 us (12%)
  matrix products  19.6 us (10%)
  local copies, waits for them, and re-layouts  17.7 us (9%)
  between operations  14.4 us (7%)
  other arithmetic  13.6 us (7%)
  starting transfers between devices  9.31 us (5%)
  Pallas kernels  8.07 us (4%)
    all_to_all x1, waiting for transfers between devices, shards(): parts = lax.all_to_all(partial, 'head', 0, 0, tiled=True)  52.9 us
    all_gather x1, waiting for transfers between devices, shards(): w_here = lax.all_gather(w_share, 'store', axis=1, tiled=True)  24.8 us
    all_to_all x1, blocking collectives, shards(): w_share = lax.all_to_all(w_share, 'head', 0, 0, tiled=True)  23.5 us
    all_to_all x1, waiting for transfers between devices, shards(): got = lax.all_to_all(sent, 'store', 0, 0, tiled=True)  13.3 us
    dot_general x1, matrix products, shards(): jnp.einsum('rf,hfc->hrc', rows, w_here, preferred_element_type=jnp.float32)  8.84 us
    pallas_call x1, Pallas kernels, page_attention(): pl.pallas_call(functools.partial(page_kernel, scale), out_shape=(jax.Shap...  8.07 us
    dot_general x1, local copies, waits for them, and re-layouts, shards(): jnp.dot(turn_rows, w_query, preferred_element_type=jnp.float32)  7.98 us
    all_to_all x1, starting transfers between devices, shards(): parts = lax.all_to_all(partial, 'head', 0, 0, tiled=True)  4.82 us
  transfers between devices with their start and end apart: 4, of which 3 were waited for; matrix products, arithmetic and copies ran while one was open for 15% of the time, Pallas kernels for 0%

profile of v2, /device:TPU:0, one launch (start us, length us, event | category | flops | bytes accessed | tf_op | source)
XLA Modules:
  0.0 197.3 jit_solution(16516689161565215807)
XLA Ops:
  6.5 1.3 dynamic-slice_bitcast_fusion
  7.9 23.5 %all_to_all.15 = bf16[4,320,256]{2,1,0:T(8,128)(2,1)} all-to-all(bf16[4,320,256]{2,1,0:T(8,128)(2,1)S(1)} %pad_maximum_fusion.1), channel_id=1, replica_groups=mesh['group'=2,'store'=4,'head'=4] {'head'}, dimensions={0} | all-to-all | bytes 1310720 | tf_op jit(solution)/shard_map/all_to_all | solution.py:96
  31.4 24.8 %all-gather.5.cloned.1.call-done = bf16[4,1280,256]{2,1,0:T(8,128)(2,1)} async-done(((bf16[4,320,256]{2,1,0:T(8,128)(2,1)}), bf16[4,1280,256]{2,1,0:T(8,128)(2,1)}) %all-gather.5.cloned.1.call-update) | async-done | bytes 2621456 | tf_op jit(solution)/shard_map/all_gather | solution.py:97
  56.3 8.8 %fusion = f16[4,1536,256]{1,2,0:T(8,128)(2,1)} fusion(bf16[4,1280,256]{2,1,0:T(8,128)(2,1)} %all-gather.5.cloned.1.call-done, bf16[1536,1280,1]{1,0,2:T(8,128)(2,1)} %bitcast.74), kind=kOutput, calls=%fused_computation.2 | convolution fusion | flops 4029677568 | bytes 9699328 | tf_op jit(solution)/shard_map/rf,hfc->hrc/dot_general | solution.py:100
  65.1 4.8 %all-to-all-start.1 = ((f16[4,1536,256]{1,2,0:T(8,128)(2,1)}), f16[4,1536,256]{1,2,0:T(8,128)(2,1)}, u32[]{:S(2)}, u32[]{:S(2)}) async-start(f16[4,1536,256]{1,2,0:T(8,128)(2,1)} %fusion), calls=%async_computation.1 | async-start | bytes 6291456 | tf_op jit(solution)/shard_map/all_to_all | solution.py:102
  70.6 8.0 %copy.49 = bf16[512,5120]{1,0:T(8,128)(2,1)} copy(bf16[512,5120]{0,1:T(8,128)(2,1)} %bitcast.63) | data formatting | bytes 10485760 | tf_op jit(solution)/shard_map/dot_general | solution.py:126
  79.3 4.1 %multiply_reduce_fusion.1 = (f32[256,4]{0,1:T(4,128)S(1)}, f32[256,4,128]{0,2,1:T(8,128)S(1)}) fusion(bf16[4,128,5120]{2,1,0:T(8,128)(2,1)} %bitcast.64, bf16[1,256,5120]{2,1,0:T(8,128)(2,1)S(1)} %copy-done), kind=kOutput, calls=%fused_computation.32 | convolution fusion | flops 1342438400 | bytes 8392704 | tf_op jit(solution)/shard_map/dot_general | solution.py:126
  85.5 3.0 %multiply_reduce_fusion.2 = (f32[256]{0:T(256)S(1)}, f32[256,128]{0,1:T(8,128)}) fusion(bf16[5120,128]{1,0:T(8,128)(2,1)} %param.12, bf16[1,256,5120]{2,1,0:T(8,128)(2,1)S(1)} %copy-done), kind=kOutput, calls=%fused_computation.44 | convolution fusion | flops 335609600 | bytes 4064256 | tf_op jit(solution)/shard_map/dot_general | solution.py:130
  88.5 52.9 %all-to-all-done.1 = f16[4,1536,256]{1,2,0:T(8,128)(2,1)} async-done(((f16[4,1536,256]{1,2,0:T(8,128)(2,1)}), f16[4,1536,256]{1,2,0:T(8,128)(2,1)}, u32[]{:S(2)}, u32[]{:S(2)}) %all-to-all-start.1) | async-done | bytes 3145760 | tf_op jit(solution)/shard_map/all_to_all | solution.py:102
  141.4 2.6 %convert_reduce_fusion = f32[1536,256]{0,1:T(8,128)S(1)} fusion(f16[4,1536,256]{1,2,0:T(8,128)(2,1)} %all-to-all-done.1), kind=kLoop, calls=%fused_computation | loop fusion | flops 2752512 | bytes 4718592 | tf_op jit(solution)/shard_map/reduce_sum | solution.py:103
  144.1 1.1 copy-done.3
  145.5 1.2 multiply_reduce_fusion
  146.8 1.3 multiply_bitcast_fusion
  148.0 1.6 fusion.22
  151.5 1.3 pad_maximum_fusion.2.k_ref
  152.9 1.2 copy-done.2
  154.1 8.1 %shard_map.91 = (bf16[4,128,1024]{2,1,0:T(8,128)(2,1)S(1)}, f32[4,8,1024]{2,1,0:T(8,128)S(1)}) custom-call(s32[24]{0:T(128)S(1)} %convert_reduce_fusion.2.session_ref, bf16[4,128,1024]{2,1,0:T(8,128)(2,1)S(1)} %copy-done.2, bf16[24,64,128]{2,1,0:T(8,128)(2,1)S(1)} %pad_maximum_fusion.2.k_ref, bf16[24,64,128]{2,1,0:T(8,128)(2,1)S(1)} %bitcast.62), custom_call_target="tpu_custom_call" | custom-call | flops 805306368 | bytes 6291456 | tf_op jit(solution)/shard_map/pallas_call | solution.py:62
  162.2 1.0 copy-done.1
  163.3 2.4 %pad_maximum_fusion = bf16[4,130,1024]{2,1,0:T(8,128)(2,1)} fusion(bf16[4,1,1024]{2,1,0:T(2,128)(2,1)S(1)} %subtract_convert_fusion.1, bf16[4,1,1024]{2,1,0:T(2,128)(2,1)S(1)} %reduce_sum.107, bf16[4,128,1024]{2,1,0:T(8,128)(2,1)} %copy-done.1), kind=kLoop, calls=%fused_computation.17 | loop fusion | flops 3194880 | bytes 2129920 | tf_op jit(solution)/shard_map/concatenate | solution.py:144
  165.7 4.4 %all-to-all-start.2 = ((bf16[4,130,1024]{2,1,0:T(8,128)(2,1)}), bf16[4,130,1024]{2,1,0:T(8,128)(2,1)}, u32[]{:S(2)}, u32[]{:S(2)}) async-start(bf16[4,130,1024]{2,1,0:T(8,128)(2,1)} %pad_maximum_fusion), calls=%async_computation.2 | async-start | bytes 2228224 | tf_op jit(solution)/shard_map/all_to_all | solution.py:145
  170.6 1.2 fusion.43
  171.9 13.3 %all-to-all-done.2 = bf16[4,130,1024]{2,1,0:T(8,128)(2,1)} async-done(((bf16[4,130,1024]{2,1,0:T(8,128)(2,1)}), bf16[4,130,1024]{2,1,0:T(8,128)(2,1)}, u32[]{:S(2)}, u32[]{:S(2)}) %all-to-all-start.2) | async-done | bytes 1064992 | tf_op jit(solution)/shard_map/all_to_all | solution.py:145
  185.2 1.5 convert_reduce_fusion.1
  186.7 2.5 %fusion.10 = bf16[128,1024]{1,0:T(8,128)(2,1)S(1)} fusion(bf16[5120,128]{1,0:T(8,128)(2,1)} %param.13, bf16[1,256,5120]{2,1,0:T(8,128)(2,1)S(1)} %copy-done, f32[130,1024]{1,0:T(8,128)S(1)} %convert_reduce_fusion.1, bf16[256,1024]{1,0:T(8,128)(2,1)} %get-tuple-element.22, f32[1024]{0:T(1024)S(1)} %bitcast.73), kind=kOutput, calls=%fused_computation.15 | convolution fusion | flops 403079168 | bytes 5246976 | tf_op jit(solution)/shard_map/kd,kc->dc/dot_general | solution.py:153
  (61 shorter events, 6.8 us)
Async XLA Ops:
  6.5 72.7 %copy-start = (bf16[1,256,5120]{2,1,0:T(8,128)(2,1)S(1)}, bf16[1,256,5120]{2,1,0:T(8,128)(2,1)}, u32[]{:S(2)}) copy-start(bf16[1,256,5120]{2,1,0:T(8,128)(2,1)} %param.10) | copy-start | bytes 7864324
  6.5 49.7 %all-gather.5.cloned.1.call-start = ((), (), s32[]{:S(2)}) async-start(), calls=%async_computation.4 | async-start | bytes 3276800 | tf_op jit(solution)/shard_map/all_gather | solution.py:97
  65.1 4.9 %copy-start.10 = (s32[4]{0:T(128)S(1)}, s32[4]{0:T(128)}, u32[]{:S(2)}) copy-start(s32[4]{0:T(128)} %param.16) | copy-start | bytes 52
  65.1 76.2 %all-to-all-start.1 = ((f16[4,1536,256]{1,2,0:T(8,128)(2,1)}), f16[4,1536,256]{1,2,0:T(8,128)(2,1)}, u32[]{:S(2)}, u32[]{:S(2)}) async-start(f16[4,1536,256]{1,2,0:T(8,128)(2,1)} %fusion), calls=%async_computation.1 | async-start | bytes 6291456 | tf_op jit(solution)/shard_map/all_to_all | solution.py:102
  69.9 82.9 %all-gather.3.cloned.1.call-start = ((), (), s32[]{:S(2)}) async-start(), calls=%async_computation.3 | async-start | bytes 1310720 | tf_op jit(solution)/shard_map/all_gather | solution.py:138
  79.3 4.4 %copy-start.9 = (f32[128]{0:T(128)S(1)}, f32[128]{0:T(128)}, u32[]{:S(2)}) copy-start(f32[128]{0:T(128)} %param.14) | copy-start | bytes 1540
  83.3 1.8 copy-start.11
  84.1 1.1 copy-start.4
  143.9 2.8 %copy-start.7 = (f32[128]{0:T(128)S(1)}, f32[128]{0:T(128)}, u32[]{:S(2)}) copy-start(f32[128]{0:T(128)} %param.15) | copy-start | bytes 1540
  144.1 1.2 copy-start.3
  152.9 1.2 copy-start.2
  162.2 1.0 copy-start.1
  163.3 6.9 %copy-start.6 = (f32[256,128]{0,1:T(8,128)S(1)}, f32[256,128]{0,1:T(8,128)}, u32[]{:S(2)}) copy-start(f32[256,128]{0,1:T(8,128)} %get-tuple-element.20) | copy-start | bytes 393220
  163.3 6.9 %copy-start.8 = (f32[128]{0:T(128)S(1)}, f32[128]{0:T(128)}, u32[]{:S(2)}) copy-start(f32[128]{0:T(128)} %param.15) | copy-start | bytes 1540
  163.3 7.3 %copy-start.5 = (bf16[128,4,256]{0,2,1:T(8,128)(2,1)S(1)}, bf16[128,4,256]{0,2,1:T(8,128)(2,1)}, u32[]{:S(2)}) copy-start(bf16[128,4,256]{0,2,1:T(8,128)(2,1)} %copy-done.4) | copy-start | bytes 786436
  165.7 19.5 %all-to-all-start.2 = ((bf16[4,130,1024]{2,1,0:T(8,128)(2,1)}), bf16[4,130,1024]{2,1,0:T(8,128)(2,1)}, u32[]{:S(2)}, u32[]{:S(2)}) async-start(bf16[4,130,1024]{2,1,0:T(8,128)(2,1)} %pad_maximum_fusion), calls=%async_computation.2 | async-start | bytes 2228224 | tf_op jit(solution)/shard_map/all_to_all | solution.py:145
Sparse Core Ops, SparseCore 0:
  31.6 24.6 all-gather.4
  85.1 17.0 all-gather.2

commit v3 on v2

--- a/solution.py
+++ b/solution.py
@@ -33,40 +33,136 @@
     )
 
 
-def page_kernel(scale, session_ref, q_ref, k_ref, v_ref, numer_ref, denom_ref, numer, denom):
-    pages = k_ref.shape[0]
-    page_len = k_ref.shape[1]
+MESH = pl.DeviceIdType.MESH
+
+
+def weight_kernel(n_head, share_ref, own_ref, out_ref, own_sem, send_sem, z_sem, x_sem, c_sem, d_sem):
+    group = lax.axis_index("group")
+    store = lax.axis_index("store")
+    head = lax.axis_index("head")
+    quarter = lax.rem(store, 4)
+    x_quarter = lax.rem(quarter + 2, 4)
+    x_mate = (group, store - quarter + x_quarter, head)
+    c_mate = (group, store + 1 - 2 * lax.rem(store, 2), head)
+
+    def head_peer(o):
+        return (group, store, lax.rem(head + o, n_head))
+
+    barrier = pltpu.get_barrier_semaphore()
+    for peer in [head_peer(o) for o in range(1, n_head)] + [x_mate, c_mate]:
+        pl.semaphore_signal(barrier, inc=1, device_id=peer, device_id_type=MESH)
+    own = pltpu.make_async_copy(own_ref, out_ref.at[head], own_sem)
+    own.start()
+    pl.semaphore_wait(barrier, n_head + 1)
+
+    sends = []
+
+    def send(src, dst, sem, kind, o, peer):
+        copy = pltpu.make_async_remote_copy(
+            src_ref=src,
+            dst_ref=dst,
+            send_sem=send_sem.at[kind, o - 1],
+            recv_sem=sem.at[o - 1],
+            device_id=peer,
+            device_id_type=MESH,
+        )
+        copy.start()
+        sends.append(copy)
+        return copy
+
+    first, second, third, fourth = {}, {}, {}, {}
+    for o in range(1, n_head):
+        target = lax.rem(head + o, n_head)
+        first[o] = send(
+            share_ref.at[target], out_ref.at[head, quarter], z_sem, 0, o, head_peer(o)
+        )
+    for o in range(1, n_head):
+        source = lax.rem(head + n_head - o, n_head)
+        first[o].wait_recv()
+        slot = out_ref.at[source, quarter]
+        second[o] = send(slot, slot, x_sem, 1, o, x_mate)
+        third[o] = send(slot, slot, c_sem, 2, o, c_mate)
+    for o in range(1, n_head):
+        source = lax.rem(head + n_head - o, n_head)
+        second[o].wait_recv()
+        slot = out_ref.at[source, x_quarter]
+        fourth[o] = send(slot, slot, d_sem, 3, o, c_mate)
+    for o in range(1, n_head):
+        third[o].wait_recv()
+        fourth[o].wait_recv()
+    for copy in sends:
+        copy.wait_send()
+    own.wait()
+
+
+def gather_weights(share, own):
+    n_head = share.shape[0]
+    return pl.pallas_call(
+        functools.partial(weight_kernel, n_head),
+        out_shape=jax.ShapeDtypeStruct((n_head,) + own.shape, share.dtype),
+        in_specs=[pl.BlockSpec(memory_space=pl.ANY)] * 2,
+        out_specs=pl.BlockSpec(memory_space=pl.ANY),
+        scratch_shapes=[
+            pltpu.SemaphoreType.DMA,
+            pltpu.SemaphoreType.DMA((4, n_head - 1)),
+            pltpu.SemaphoreType.DMA((n_head - 1,)),
+            pltpu.SemaphoreType.DMA((n_head - 1,)),
+            pltpu.SemaphoreType.DMA((n_head - 1,)),
+            pltpu.SemaphoreType.DMA((n_head - 1,)),
+        ],
+        compiler_params=pltpu.CompilerParams(collective_id=0, has_side_effects=True),
+        cost_estimate=pl.CostEstimate(flops=0, bytes_accessed=4 << 20, transcendentals=0),
+    )(share, own)
+
+
+def page_kernel(
+    scale, n_block, session_ref, q_ref, gain_ref, cos_ref, sin_ref, *refs
+):
+    pair_refs = refs[:n_block]
+    numer_ref, denom_ref, numer, denom = refs[n_block:]
+    page_len, head_dim = cos_ref.shape[1:]
     numer[...] = jnp.zeros_like(numer)
     denom[...] = jnp.zeros_like(denom)
-
-    def body(p, carry):
-        s = session_ref[p]
-        scores = jnp.dot(k_ref[p], q_ref[s], preferred_element_type=jnp.float32)
-        weight = jnp.exp(scores * scale)
-        denom[s] += jnp.sum(weight.reshape(page_len // 8, 8, weight.shape[-1]), axis=0)
-        numer[s] += lax.dot_general(
-            v_ref[p],
-            weight.astype(jnp.bfloat16),
-            (((0,), (0,)), ((), ())),
-            preferred_element_type=jnp.float32,
-        )
-        return carry
-
-    lax.fori_loop(0, pages, body, 0, unroll=2)
+    gain = gain_ref[...]
+
+    for block, pair_ref in enumerate(pair_refs):
+        pages = pair_ref.shape[0]
+
+        def body(i, carry):
+            p = block * pages + i
+            s = session_ref[p]
+            raw = pair_ref[i, :, :head_dim]
+            mean_sq = jnp.mean(raw * raw, axis=-1, keepdims=True)
+            normed = raw * lax.rsqrt(mean_sq + epsilon) * gain
+            turned = pltpu.roll(normed, head_dim // 2, 1)
+            keys = (normed * cos_ref[p] + turned * sin_ref[p]).astype(jnp.bfloat16)
+            values = pair_ref[i, :, head_dim:].astype(jnp.bfloat16)
+            scores = jnp.dot(keys, q_ref[s], preferred_element_type=jnp.float32)
+            weight = jnp.exp(scores * scale)
+            denom[s] += jnp.sum(weight.reshape(page_len // 8, 8, weight.shape[-1]), axis=0)
+            numer[s] += lax.dot_general(
+                values,
+                weight.astype(jnp.bfloat16),
+                (((0,), (0,)), ((), ())),
+                preferred_element_type=jnp.float32,
+            )
+            return carry
+
+        lax.fori_loop(0, pages, body, 0, unroll=2)
     numer_ref[...] = numer[...].astype(jnp.bfloat16)
     denom_ref[...] = denom[...]
 
 
-def page_attention(session_of, queries, keys, values, scale):
+def page_attention(session_of, queries, gain, cosine, sine, pairs, scale):
     sess_count, head_dim, columns = queries.shape
     return pl.pallas_call(
-        functools.partial(page_kernel, scale),
+        functools.partial(page_kernel, scale, len(pairs)),
         out_shape=(
             jax.ShapeDtypeStruct((sess_count, head_dim, columns), jnp.bfloat16),
             jax.ShapeDtypeStruct((sess_count, 8, columns), jnp.float32),
         ),
         in_specs=[pl.BlockSpec(memory_space=pltpu.SMEM)]
-        + [pl.BlockSpec(memory_space=pltpu.VMEM)] * 3,
+        + [pl.BlockSpec(memory_space=pltpu.VMEM)] * (4 + len(pairs)),
         out_specs=[pl.BlockSpec(memory_space=pltpu.VMEM)] * 2,
         scratch_shapes=[
             pltpu.VMEM((sess_count, head_dim, columns), jnp.float32),
@@ -74,9 +170,9 @@
         ],
         compiler_params=pltpu.CompilerParams(vmem_limit_bytes=48 * 1024 * 1024),
         cost_estimate=pl.CostEstimate(
-            flops=4 * keys.size * columns, bytes_accessed=6 << 20, transcendentals=0
+            flops=4 * cosine.size * columns, bytes_accessed=6 << 20, transcendentals=0
         ),
-    )(session_of, queries, keys, values)
+    )(session_of, queries, gain[None, :], cosine, sine, *pairs)
 
 
 def shards(saved, fresh, w_query, w_key, w_value, q_gain, k_gain, lengths, slot_page):
@@ -86,21 +182,46 @@
     n_store = lax.axis_size("store")
     my_store = lax.axis_index("store")
     sess_count = lengths.shape[0]
-    share = part_width // n_store
-
-    def my_rows(w):
-        cut = w.reshape(n_head, n_store, share, head_dim)
-        return lax.dynamic_index_in_dim(cut, my_store, 1, keepdims=False)
-
-    w_share = jnp.concatenate([my_rows(w_key), my_rows(w_value)], axis=2)
-    w_share = lax.all_to_all(w_share, "head", 0, 0, tiled=True)
-    w_here = lax.all_gather(w_share, "store", axis=1, tiled=True)
-    rows = saved.reshape(-1, part_width)
-    partial = (
-        jnp.einsum("rf,hfc->hrc", rows, w_here, preferred_element_type=jnp.float32) * part_scale
-    ).astype(jnp.float16)
-    parts = lax.all_to_all(partial, "head", 0, 0, tiled=True)
-    pair = jnp.sum(parts.astype(jnp.float32), axis=0) * (1.0 / part_scale)
+    head = lax.axis_index("head")
+    w_pair = jnp.concatenate([w_key, w_value], axis=1).reshape(
+        n_head, 4, part_width // 4, 2 * head_dim
+    )
+    w_share = lax.dynamic_index_in_dim(w_pair, lax.rem(my_store, 4), 1, keepdims=False)
+    w_own = lax.dynamic_index_in_dim(w_pair, head, 0, keepdims=False)
+    w_here = gather_weights(w_share, w_own).reshape(n_head, part_width, 2 * head_dim)
+
+    n_block = 2 if page_count % 2 == 0 else 1
+    block_pages = page_count // n_block
+    blocks = [
+        saved[i * block_pages : (i + 1) * block_pages].reshape(-1, part_width)
+        for i in range(n_block)
+    ]
+
+    def product(block, target):
+        weights = lax.dynamic_index_in_dim(w_here, target, 0, keepdims=False)
+        return jnp.dot(block, weights, preferred_element_type=jnp.float32) * part_scale
+
+    ups = [None] * n_block
+    downs = [None] * n_block
+    for r in range(n_head - 1):
+        up_to = jnp.minimum(n_head - 1 - r + head, n_head - 1)
+        down_to = jnp.maximum(r - (n_head - 1) + head, 0)
+        up_pairs = [(i, i + 1) for i in range(r + 1)]
+        down_pairs = [(n_head - 1 - i, n_head - 2 - i) for i in range(r + 1)]
+        for i, block in enumerate(blocks):
+            up = product(block, up_to)
+            down = product(block, down_to)
+            if r > 0:
+                up = up + ups[i].astype(jnp.float32)
+                down = down + downs[i].astype(jnp.float32)
+            ups[i] = lax.ppermute(up.astype(jnp.float16), "head", up_pairs)
+            downs[i] = lax.ppermute(down.astype(jnp.float16), "head", down_pairs)
+    pairs = []
+    for i, block in enumerate(blocks):
+        total = product(block, head) + (
+            ups[i].astype(jnp.float32) + downs[i].astype(jnp.float32)
+        )
+        pairs.append((total * (1.0 / part_scale)).reshape(block_pages, page_len, 2 * head_dim))
 
     ends = jnp.cumsum(lengths)
     starts = ends - lengths
@@ -112,11 +233,14 @@
     key_pos = ((slot_page - first_page) * page_len)[:, None] + jnp.arange(
         page_len, dtype=jnp.int32
     )[None, :]
-    keys = rotary(head_norm(pair[:, None, :head_dim], k_gain), key_pos.reshape(-1)).astype(
-        jnp.bfloat16
-    )
-    keys = keys.reshape(page_count, page_len, head_dim)
-    values = pair[:, head_dim:].astype(jnp.bfloat16).reshape(page_count, page_len, head_dim)
+    half = head_dim // 2
+    freqs = jnp.exp(
+        -jnp.arange(half, dtype=jnp.float32) * (2.0 / head_dim) * math.log(rope_base)
+    )
+    angles = key_pos.astype(jnp.float32)[:, :, None] * freqs[None, None, :]
+    cosine, sine = jnp.cos(angles), jnp.sin(angles)
+    cosine = jnp.concatenate([cosine, cosine], axis=-1)
+    sine = jnp.concatenate([-sine, sine], axis=-1)
 
     turn_rows = fresh[0]
     new_count = turn_rows.shape[0]
@@ -137,7 +261,9 @@
     q_t = queries.transpose(2, 1, 0).reshape(head_dim, columns)
     every_query = lax.all_gather(q_t, "store", axis=0)
 
-    numer_t, denom_8 = page_attention(session_of, every_query, keys, values, scale)
+    numer_t, denom_8 = page_attention(
+        session_of, every_query, k_gain, cosine, sine, pairs, scale
+    )
     denom = jnp.sum(denom_8, axis=1)
     high = denom.astype(jnp.bfloat16)
     low = (denom - high.astype(jnp.float32)).astype(jnp.bfloat16)

time: 198 us -> 203 us (1.025)
  waiting for transfers between devices: 91.1 us -> 20.8 us
  Pallas kernels: 8.07 us -> 37.6 us
  matrix products: 19.6 us -> 47.3 us
  blocking collectives: 23.5 us -> 0 us
  starting transfers between devices: 9.31 us -> 32.2 us
  local copies, waits for them, and re-layouts: 17.7 us -> 28.8 us
  other arithmetic: 13.6 us -> 19 us
    all_to_all x1 -> x0, waiting for transfers between devices: 52.9 us -> none  [shards(): parts = lax.all_to_all(partial, 'head', 0, 0, tiled=True)]
    pallas_call x1 -> x2, Pallas kernels: 8.07 us -> 37.6 us  [the longest x1 27.8 us: gather_weights(): pl.pallas_call(functools.partial(weight_kernel, n_head), out_shape=jax.Sh...]
    dot_general x1 -> x14, matrix products: 8.84 us -> 37.8 us  [product(): jnp.dot(block, weights, preferred_element_type=jnp.float32) * part_scale]
    ppermute x0 -> x12, starting transfers between devices: none -> 27.9 us  [the longest x6 20.7 us: shards(): ups[i] = lax.ppermute(up.astype(jnp.float16), 'head', up_pairs)]
    all_gather x1 -> x0, waiting for transfers between devices: 24.8 us -> none  [shards(): w_here = lax.all_gather(w_share, 'store', axis=1, tiled=True)]
    all_to_all x1 -> x0, blocking collectives: 23.5 us -> none  [shards(): w_share = lax.all_to_all(w_share, 'head', 0, 0, tiled=True)]
    ppermute x0 -> x12, waiting for transfers between devices: none -> 7.25 us  [the longest x6 3.9 us: shards(): downs[i] = lax.ppermute(down.astype(jnp.float16), 'head', down_pairs)]
    all_to_all x1 -> x0, starting transfers between devices: 4.82 us -> none  [shards(): parts = lax.all_to_all(partial, 'head', 0, 0, tiled=True)]
  transfers between devices with their start and end apart: 4 -> 14, of which waited for: 3 -> 5; matrix products, arithmetic and copies ran while one was open for 15% -> 34% of each run, Pallas kernels for 0% -> 0%
where the time goes in v3:
time: 203 us; the launch traced here: 200 us
  matrix products  47.3 us (23%)
  Pallas kernels  37.6 us (19%)
  starting transfers between devices  32.2 us (16%)
  local copies, waits for them, and re-layouts  28.8 us (14%)
  waiting for transfers between devices  20.8 us (10%)
  other arithmetic  19 us (9%)
  between operations  14.6 us (7%)
    dot_general x14, matrix products, product(): jnp.dot(block, weights, preferred_element_type=jnp.float32) * part_scale  37.8 us
    pallas_call x1, Pallas kernels, gather_weights(): pl.pallas_call(functools.partial(weight_kernel, n_head), out_shape=jax.Sh...  27.8 us
    ppermute x6, starting transfers between devices, shards(): ups[i] = lax.ppermute(up.astype(jnp.float16), 'head', up_pairs)  20.7 us
    all_to_all x1, waiting for transfers between devices, shards(): got = lax.all_to_all(sent, 'store', 0, 0, tiled=True)  13.5 us
    pallas_call x1, Pallas kernels, page_attention(): pl.pallas_call(functools.partial(page_kernel, scale, len(pairs)), out_sha...  9.79 us
    dot_general x1, local copies, waits for them, and re-layouts, shards(): jnp.dot(turn_rows, w_query, preferred_element_type=jnp.float32)  7.84 us
    ppermute x6, starting transfers between devices, shards(): downs[i] = lax.ppermute(down.astype(jnp.float16), 'head', down_pairs)  7.24 us
    unnamed x60, local copies, waits for them, and re-layouts  7.18 us
  transfers between devices with their start and end apart: 14, of which 5 were waited for; matrix products, arithmetic and copies ran while one was open for 34% of the time, Pallas kernels for 0%

profile of v3, /device:TPU:0, one launch (start us, length us, event | category | flops | bytes accessed | tf_op | source)
XLA Modules:
  0.0 200.3 jit_solution(11006207956816999319)
XLA Ops:
  13.0 4.5 %fusion.103 = (bf16[12,64,1280]{2,1,0:T(8,128)(2,1)}, bf16[12,64,1280]{2,1,0:T(8,128)(2,1)}) fusion(bf16[24,64,1280]{2,1,0:T(8,128)(2,1)} %param.9), kind=kLoop, calls=%fused_computation.154 | loop fusion | bytes 7864320 | tf_op jit(solution)/shard_map/slice | solution.py:196
  17.5 27.8 %shard_map.91 = bf16[4,4,320,256]{3,2,1,0:T(8,128)(2,1)} custom-call(bf16[4,320,256]{2,1,0:T(8,128)(2,1)} %dynamic-slice_bitcast_fusion.1.share_ref, bf16[4,320,256]{2,1,0:T(8,128)(2,1)} %dynamic-slice_bitcast_fusion.own_ref), custom_call_target="tpu_custom_call" | custom-call | bytes 4194304 | tf_op jit(solution)/shard_map/pallas_call | solution.py:100
  45.3 3.3 %fusion.25 = f16[768,256]{0,1:T(8,128)(2,1)} fusion(bf16[768,1280]{1,0:T(8,128)(2,1)} %bitcast.154, bf16[4,1280,256]{2,1,0:T(8,128)(2,1)} %bitcast.161, s32[]{:T(128)S(6)} %select_n.53), kind=kOutput, calls=%fused_computation.43 | convolution fusion | flops 503709696 | bytes 3014660 | tf_op jit(solution)/shard_map/dot_general | solution.py:202
  48.5 3.2 %collective-permute-start.6 = (f16[768,256]{0,1:T(8,128)(2,1)}, f16[768,256]{0,1:T(8,128)(2,1)}, u32[]{:S(2)}, u32[]{:S(2)}) collective-permute-start(f16[768,256]{0,1:T(8,128)(2,1)} %fusion.25), channel_id=1, source_target_pairs={{0,1},{4,5},{8,9},{12,13},{16,17},{20,21},{24,25},{28,29}} | collective-permute-start | bytes 1179656 | tf_op jit(solution)/shard_map/ppermute | solution.py:217
  51.8 3.4 %fusion.24 = f16[768,256]{0,1:T(8,128)(2,1)} fusion(bf16[768,1280]{1,0:T(8,128)(2,1)} %bitcast.155, bf16[4,1280,256]{2,1,0:T(8,128)(2,1)} %bitcast.162, s32[]{:T(128)S(6)} %max.11), kind=kOutput, calls=%fused_computation.42 | convolution fusion | flops 503709696 | bytes 3014660 | tf_op jit(solution)/shard_map/dot_general | solution.py:202
  56.5 2.6 %fusion.27 = f16[768,256]{0,1:T(8,128)(2,1)} fusion(bf16[768,1280]{1,0:T(8,128)(2,1)S(1)} %bitcast.147, bf16[4,1280,256]{2,1,0:T(8,128)(2,1)} %bitcast.163, s32[]{:T(128)S(6)} %select_n.53), kind=kOutput, calls=%fused_computation.45 | convolution fusion | flops 503709696 | bytes 3014660 | tf_op jit(solution)/shard_map/dot_general | solution.py:202
  61.3 2.6 %fusion.26 = f16[768,256]{0,1:T(8,128)(2,1)} fusion(bf16[768,1280]{1,0:T(8,128)(2,1)S(1)} %bitcast.148, bf16[4,1280,256]{2,1,0:T(8,128)(2,1)} %bitcast.164, s32[]{:T(128)S(6)} %max.11), kind=kOutput, calls=%fused_computation.44 | convolution fusion | flops 503709696 | bytes 3014660 | tf_op jit(solution)/shard_map/dot_general | solution.py:202
  66.6 7.8 %copy.40 = bf16[512,5120]{1,0:T(8,128)(2,1)} copy(bf16[512,5120]{0,1:T(8,128)(2,1)} %bitcast.177) | data formatting | bytes 10485760 | tf_op jit(solution)/shard_map/dot_general | solution.py:250
  74.4 4.1 %multiply_reduce_fusion = (f32[256,4]{0,1:T(4,128)S(1)}, f32[256,4,128]{0,2,1:T(8,128)S(1)}) fusion(bf16[4,128,5120]{2,1,0:T(8,128)(2,1)} %bitcast.178, bf16[1,256,5120]{2,1,0:T(8,128)(2,1)S(1)} %copy-done), kind=kOutput, calls=%fused_computation.95 | convolution fusion | flops 1342438400 | bytes 8392704 | tf_op jit(solution)/shard_map/dot_general | solution.py:250
  80.1 3.4 %fusion.12 = f32[768,256]{0,1:T(8,128)} fusion(bf16[768,1280]{1,0:T(8,128)(2,1)} %bitcast.156, bf16[4,1280,256]{2,1,0:T(8,128)(2,1)} %bitcast.165, s32[]{:T(128)S(6)} %select_n.50), kind=kOutput, calls=%fused_computation.22 | convolution fusion | flops 503513088 | bytes 3407876 | tf_op jit(solution)/shard_map/dot_general | solution.py:202
  83.5 3.5 %fusion.11 = f32[768,256]{0,1:T(8,128)} fusion(bf16[768,1280]{1,0:T(8,128)(2,1)} %bitcast.157, bf16[4,1280,256]{2,1,0:T(8,128)(2,1)} %bitcast.166, s32[]{:T(128)S(6)} %select_n.51), kind=kOutput, calls=%fused_computation.20 | convolution fusion | flops 503513088 | bytes 3407876 | tf_op jit(solution)/shard_map/dot_general | solution.py:202
  87.1 2.8 %fusion.16 = f32[768,256]{0,1:T(8,128)} fusion(bf16[768,1280]{1,0:T(8,128)(2,1)S(1)} %bitcast.149, bf16[4,1280,256]{2,1,0:T(8,128)(2,1)} %bitcast.167, s32[]{:T(128)S(6)} %select_n.51), kind=kOutput, calls=%fused_computation.32 | convolution fusion | flops 503513088 | bytes 3407876 | tf_op jit(solution)/shard_map/dot_general | solution.py:202
  89.8 3.5 %fusion.9 = f32[768,256]{0,1:T(8,128)} fusion(bf16[768,1280]{1,0:T(8,128)(2,1)} %bitcast.158, bf16[4,1280,256]{2,1,0:T(8,128)(2,1)} %bitcast.168, s32[]{:T(128)S(6)} %max.9), kind=kOutput, calls=%fused_computation.15 | convolution fusion | flops 503513088 | bytes 3407876 | tf_op jit(solution)/shard_map/dot_general | solution.py:202
  95.2 2.8 %fusion.17 = f32[768,256]{0,1:T(8,128)} fusion(bf16[768,1280]{1,0:T(8,128)(2,1)S(1)} %bitcast.151, bf16[4,1280,256]{2,1,0:T(8,128)(2,1)} %bitcast.170, s32[]{:T(128)S(6)} %select_n.50), kind=kOutput, calls=%fused_computation.34 | convolution fusion | flops 503513088 | bytes 3407876 | tf_op jit(solution)/shard_map/dot_general | solution.py:202
  100.2 4.5 %fusion.70 = (f32[24,64,64]{2,1,0:T(8,128)}, f32[24,64,64]{2,1,0:T(8,128)}, f32[24,64,64]{2,1,0:T(8,128)}) fusion(f32[64]{0:T(128)S(1)} %multiply_exponential_fusion, f32[24,64]{1,0:T(8,128)S(1)} %add_convert_fusion.9), kind=kLoop, calls=%fused_computation.99 | loop fusion | flops 196608 | bytes 1186048 | tf_op jit(solution)/shard_map/neg | solution.py:243
  104.7 2.7 %add_convert_fusion.3 = f16[768,256]{0,1:T(8,128)(2,1)S(1)} fusion(f16[768,256]{0,1:T(8,128)(2,1)} %collective-permute-done.6, bf16[768,1280]{1,0:T(8,128)(2,1)} %bitcast.159, bf16[4,1280,256]{2,1,0:T(8,128)(2,1)} %bitcast.171, s32[]{:T(128)S(6)} %select_n.52), kind=kOutput, calls=%fused_computation.57 | convolution fusion | flops 504102912 | bytes 3407876 | tf_op jit(solution)/shard_map/dot_general | solution.py:202
  113.3 3.3 %collective-permute-start.1 = (f16[768,256]{0,1:T(8,128)(2,1)S(1)}, f16[768,256]{0,1:T(8,128)(2,1)S(1)}, u32[]{:S(2)}, u32[]{:S(2)}) collective-permute-start(f16[768,256]{0,1:T(8,128)(2,1)S(1)} %add_convert_fusion.7), channel_id=1, source_target_pairs={{0,1},{1,2},{4,5},{5,6},{8,9},{9,10},{12,13},{13,14},{16,17},{17,1... | collective-permute-start | bytes 1179656 | tf_op jit(solution)/shard_map/ppermute | solution.py:217
  119.4 5.2 %collective-permute-start.8 = (f16[768,256]{0,1:T(8,128)(2,1)S(1)}, f16[768,256]{0,1:T(8,128)(2,1)S(1)}, u32[]{:S(2)}, u32[]{:S(2)}) collective-permute-start(f16[768,256]{0,1:T(8,128)(2,1)S(1)} %add_convert_fusion.2), channel_id=1, source_target_pairs={{0,1},{1,2},{2,3},{4,5},{5,6},{6,7},{8,9},{9,10},{10,11},{12,13},{... | collective-permute-start | bytes 1179656 | tf_op jit(solution)/shard_map/ppermute | solution.py:217
  127.6 5.4 %collective-permute-start.2 = (f16[768,256]{0,1:T(8,128)(2,1)}, f16[768,256]{0,1:T(8,128)(2,1)}, u32[]{:S(2)}, u32[]{:S(2)}) collective-permute-start(f16[768,256]{0,1:T(8,128)(2,1)} %add_convert_fusion.6), channel_id=1, source_target_pairs={{0,1},{1,2},{2,3},{4,5},{5,6},{6,7},{8,9},{9,10},{10,11},{12,13},{... | collective-permute-start | bytes 1179656 | tf_op jit(solution)/shard_map/ppermute | solution.py:217
  140.3 2.8 %collective-permute-done.2 = f16[768,256]{0,1:T(8,128)(2,1)} collective-permute-done((f16[768,256]{0,1:T(8,128)(2,1)}, f16[768,256]{0,1:T(8,128)(2,1)}, u32[]{:S(2)}, u32[]{:S(2)}) %collective-permute-start.2) | collective-permute-done | bytes 393248 | tf_op jit(solution)/shard_map/ppermute | solution.py:217
  143.1 3.0 %collective-permute-done.5 = f16[768,256]{0,1:T(8,128)(2,1)} collective-permute-done((f16[768,256]{0,1:T(8,128)(2,1)}, f16[768,256]{0,1:T(8,128)(2,1)}, u32[]{:S(2)}, u32[]{:S(2)}) %collective-permute-start.5) | collective-permute-done | bytes 393248 | tf_op jit(solution)/shard_map/ppermute | solution.py:218
  155.4 9.8 %shard_map.92 = (bf16[4,128,1024]{2,1,0:T(8,128)(2,1)S(1)}, f32[4,8,1024]{2,1,0:T(8,128)S(1)}) custom-call(s32[24]{0:T(128)S(1)} %convert_reduce_fusion.1.session_ref, bf16[4,128,1024]{2,1,0:T(8,128)(2,1)S(1)} %copy-done.4, f32[1,128]{1,0:T(1,128)S(1)} %bitcast.146, f32[24,64,128]{2,1,0:T(8,128)S(1)} %copy-done.2, f32[24,64,128]{2,1,0:T(8,128)S(1)} %copy-done.3, ...), custom_call_target="tpu_custom_call" | custom-call | flops 805306368 | bytes 6291456 | tf_op jit(solution)/shard_map/pallas_call | solution.py:158
  168.7 4.2 %all-to-all-start = ((bf16[4,130,1024]{2,1,0:T(8,128)(2,1)}), bf16[4,130,1024]{2,1,0:T(8,128)(2,1)}, u32[]{:S(2)}, u32[]{:S(2)}) async-start(bf16[4,130,1024]{2,1,0:T(8,128)(2,1)} %pad_maximum_fusion.1), calls=%async_computation | async-start | bytes 2228224 | tf_op jit(solution)/shard_map/all_to_all | solution.py:271
  174.7 13.5 %all-to-all-done = bf16[4,130,1024]{2,1,0:T(8,128)(2,1)} async-done(((bf16[4,130,1024]{2,1,0:T(8,128)(2,1)}), bf16[4,130,1024]{2,1,0:T(8,128)(2,1)}, u32[]{:S(2)}, u32[]{:S(2)}) %all-to-all-start) | async-done | bytes 1064992 | tf_op jit(solution)/shard_map/all_to_all | solution.py:271
  (130 shorter events, 56.1 us)
Async XLA Ops:
  6.5 67.9 %copy-start = (bf16[1,256,5120]{2,1,0:T(8,128)(2,1)S(1)}, bf16[1,256,5120]{2,1,0:T(8,128)(2,1)}, u32[]{:S(2)}) copy-start(bf16[1,256,5120]{2,1,0:T(8,128)(2,1)} %param.10) | copy-start | bytes 7864324
  6.5 144.2 %all-gather.2.cloned.1.call-start = ((), (), s32[]{:S(2)}) async-start(), calls=%async_computation.1 | async-start | bytes 1310720 | tf_op jit(solution)/shard_map/all_gather | solution.py:262
  48.5 56.2 %collective-permute-start.6 = (f16[768,256]{0,1:T(8,128)(2,1)}, f16[768,256]{0,1:T(8,128)(2,1)}, u32[]{:S(2)}, u32[]{:S(2)}) collective-permute-start(f16[768,256]{0,1:T(8,128)(2,1)} %fusion.25), channel_id=1, source_target_pairs={{0,1},{4,5},{8,9},{12,13},{16,17},{20,21},{24,25},{28,29}} | collective-permute-start | bytes 1179656 | tf_op jit(solution)/shard_map/ppermute | solution.py:217
  55.1 53.7 %collective-permute-start.9 = (f16[768,256]{0,1:T(8,128)(2,1)}, f16[768,256]{0,1:T(8,128)(2,1)}, u32[]{:S(2)}, u32[]{:S(2)}) collective-permute-start(f16[768,256]{0,1:T(8,128)(2,1)} %fusion.24), channel_id=1, source_target_pairs={{3,2},{7,6},{11,10},{15,14},{19,18},{23,22},{27,26},{31,30}} | collective-permute-start | bytes 1179656 | tf_op jit(solution)/shard_map/ppermute | solution.py:218
  59.1 52.4 %collective-permute-start = (f16[768,256]{0,1:T(8,128)(2,1)}, f16[768,256]{0,1:T(8,128)(2,1)}, u32[]{:S(2)}, u32[]{:S(2)}) collective-permute-start(f16[768,256]{0,1:T(8,128)(2,1)} %fusion.27), channel_id=1, source_target_pairs={{0,1},{4,5},{8,9},{12,13},{16,17},{20,21},{24,25},{28,29}} | collective-permute-start | bytes 1179656 | tf_op jit(solution)/shard_map/ppermute | solution.py:217
  63.9 52.7 %collective-permute-start.3 = (f16[768,256]{0,1:T(8,128)(2,1)}, f16[768,256]{0,1:T(8,128)(2,1)}, u32[]{:S(2)}, u32[]{:S(2)}) collective-permute-start(f16[768,256]{0,1:T(8,128)(2,1)} %fusion.26), channel_id=1, source_target_pairs={{3,2},{7,6},{11,10},{15,14},{19,18},{23,22},{27,26},{31,30}} | collective-permute-start | bytes 1179656 | tf_op jit(solution)/shard_map/ppermute | solution.py:218
  65.3 13.2 %copy-start.25 = (f32[64]{0:T(128)}, f32[64]{0:T(128)S(1)}, u32[]{:S(2)}) copy-start(f32[64]{0:T(128)S(1)} %multiply_exponential_fusion.1) | copy-start | bytes 772
  104.7 6.8 %copy-start.12 = (bf16[4,4,320,256]{3,2,1,0:T(8,128)(2,1)S(1)}, bf16[4,4,320,256]{3,2,1,0:T(8,128)(2,1)}, u32[]{:S(2)}) copy-start(bf16[4,4,320,256]{3,2,1,0:T(8,128)(2,1)} %shard_map.91) | copy-start | bytes 7864324
  107.4 11.8 %collective-permute-start.7 = (f16[768,256]{0,1:T(8,128)(2,1)S(1)}, f16[768,256]{0,1:T(8,128)(2,1)S(1)}, u32[]{:S(2)}, u32[]{:S(2)}) collective-permute-start(f16[768,256]{0,1:T(8,128)(2,1)S(1)} %add_convert_fusion.3), channel_id=1, source_target_pairs={{0,1},{1,2},{4,5},{5,6},{8,9},{9,10},{12,13},{13,14},{16,17},{17,1... | collective-permute-start | bytes 1179656 | tf_op jit(solution)/shard_map/ppermute | solution.py:217
  110.8 13.7 %collective-permute-start.10 = (f16[768,256]{0,1:T(8,128)(2,1)S(1)}, f16[768,256]{0,1:T(8,128)(2,1)S(1)}, u32[]{:S(2)}, u32[]{:S(2)}) collective-permute-start(f16[768,256]{0,1:T(8,128)(2,1)S(1)} %add_convert_fusion.1), channel_id=1, source_target_pairs={{3,2},{2,1},{7,6},{6,5},{11,10},{10,9},{15,14},{14,13},{19,18},{18... | collective-permute-start | bytes 1179656 | tf_op jit(solution)/shard_map/ppermute | solution.py:218
  113.3 11.2 %copy-start.16 = (f32[768,256]{0,1:T(8,128)S(1)}, f32[768,256]{0,1:T(8,128)}, u32[]{:S(2)}) copy-start(f32[768,256]{0,1:T(8,128)} %fusion.9) | copy-start | bytes 2359300
  113.3 13.4 %collective-permute-start.1 = (f16[768,256]{0,1:T(8,128)(2,1)S(1)}, f16[768,256]{0,1:T(8,128)(2,1)S(1)}, u32[]{:S(2)}, u32[]{:S(2)}) collective-permute-start(f16[768,256]{0,1:T(8,128)(2,1)S(1)} %add_convert_fusion.7), channel_id=1, source_target_pairs={{0,1},{1,2},{4,5},{5,6},{8,9},{9,10},{12,13},{13,14},{16,17},{17,1... | collective-permute-start | bytes 1179656 | tf_op jit(solution)/shard_map/ppermute | solution.py:217
  118.4 8.3 %copy-start.15 = (f32[768,256]{0,1:T(8,128)S(1)}, f32[768,256]{0,1:T(8,128)}, u32[]{:S(2)}) copy-start(f32[768,256]{0,1:T(8,128)} %fusion.16) | copy-start | bytes 2359300
  118.4 14.5 %collective-permute-start.4 = (f16[768,256]{0,1:T(8,128)(2,1)S(1)}, f16[768,256]{0,1:T(8,128)(2,1)S(1)}, u32[]{:S(2)}, u32[]{:S(2)}) collective-permute-start(f16[768,256]{0,1:T(8,128)(2,1)S(1)} %add_convert_fusion.5), channel_id=1, source_target_pairs={{3,2},{2,1},{7,6},{6,5},{11,10},{10,9},{15,14},{14,13},{19,18},{18... | collective-permute-start | bytes 1179656 | tf_op jit(solution)/shard_map/ppermute | solution.py:218
  119.4 17.7 %collective-permute-start.8 = (f16[768,256]{0,1:T(8,128)(2,1)S(1)}, f16[768,256]{0,1:T(8,128)(2,1)S(1)}, u32[]{:S(2)}, u32[]{:S(2)}) collective-permute-start(f16[768,256]{0,1:T(8,128)(2,1)S(1)} %add_convert_fusion.2), channel_id=1, source_target_pairs={{0,1},{1,2},{2,3},{4,5},{5,6},{6,7},{8,9},{9,10},{10,11},{12,13},{... | collective-permute-start | bytes 1179656 | tf_op jit(solution)/shard_map/ppermute | solution.py:217
  124.7 10.7 %copy-start.19 = (f32[24,64,64]{2,1,0:T(8,128)S(1)}, f32[24,64,64]{2,1,0:T(8,128)}, u32[]{:S(2)}) copy-start(f32[24,64,64]{2,1,0:T(8,128)} %get-tuple-element.15) | copy-start | bytes 1179652
  124.7 10.7 %copy-start.20 = (f32[24,64,64]{2,1,0:T(8,128)S(1)}, f32[24,64,64]{2,1,0:T(8,128)}, u32[]{:S(2)}) copy-start(f32[24,64,64]{2,1,0:T(8,128)} %get-tuple-element.16) | copy-start | bytes 1179652
  124.7 10.7 %copy-start.21 = (f32[24,64,64]{2,1,0:T(8,128)S(1)}, f32[24,64,64]{2,1,0:T(8,128)}, u32[]{:S(2)}) copy-start(f32[24,64,64]{2,1,0:T(8,128)} %get-tuple-element.17) | copy-start | bytes 1179652
  124.7 13.2 %collective-permute-start.11 = (f16[768,256]{0,1:T(8,128)(2,1)S(1)}, f16[768,256]{0,1:T(8,128)(2,1)S(1)}, u32[]{:S(2)}, u32[]{:S(2)}) collective-permute-start(f16[768,256]{0,1:T(8,128)(2,1)S(1)} %add_convert_fusion), channel_id=1, source_target_pairs={{3,2},{2,1},{1,0},{7,6},{6,5},{5,4},{11,10},{10,9},{9,8},{15,14},{... | collective-permute-start | bytes 1179656 | tf_op jit(solution)/shard_map/ppermute | solution.py:218
  127.6 15.5 %collective-permute-start.2 = (f16[768,256]{0,1:T(8,128)(2,1)}, f16[768,256]{0,1:T(8,128)(2,1)}, u32[]{:S(2)}, u32[]{:S(2)}) collective-permute-start(f16[768,256]{0,1:T(8,128)(2,1)} %add_convert_fusion.6), channel_id=1, source_target_pairs={{0,1},{1,2},{2,3},{4,5},{5,6},{6,7},{8,9},{9,10},{10,11},{12,13},{... | collective-permute-start | bytes 1179656 | tf_op jit(solution)/shard_map/ppermute | solution.py:217
  133.8 12.3 %collective-permute-start.5 = (f16[768,256]{0,1:T(8,128)(2,1)}, f16[768,256]{0,1:T(8,128)(2,1)}, u32[]{:S(2)}, u32[]{:S(2)}) collective-permute-start(f16[768,256]{0,1:T(8,128)(2,1)} %add_convert_fusion.4), channel_id=1, source_target_pairs={{3,2},{2,1},{1,0},{7,6},{6,5},{5,4},{11,10},{10,9},{9,8},{15,14},{... | collective-permute-start | bytes 1179656 | tf_op jit(solution)/shard_map/ppermute | solution.py:218
  140.3 10.5 %copy-start.6 = (f32[128]{0:T(128)S(1)}, f32[128]{0:T(128)}, u32[]{:S(2)}) copy-start(f32[128]{0:T(128)} %param.15) | copy-start | bytes 1540
  166.3 7.1 %copy-start.23 = (bf16[128,4,256]{0,2,1:T(8,128)(2,1)S(1)}, bf16[128,4,256]{0,2,1:T(8,128)(2,1)}, u32[]{:S(2)}) copy-start(bf16[128,4,256]{0,2,1:T(8,128)(2,1)} %copy-done.22) | copy-start | bytes 786436
  168.7 19.5 %all-to-all-start = ((bf16[4,130,1024]{2,1,0:T(8,128)(2,1)}), bf16[4,130,1024]{2,1,0:T(8,128)(2,1)}, u32[]{:S(2)}, u32[]{:S(2)}) async-start(bf16[4,130,1024]{2,1,0:T(8,128)(2,1)} %pad_maximum_fusion.1), calls=%async_computation | async-start | bytes 2228224 | tf_op jit(solution)/shard_map/all_to_all | solution.py:271
  (20 other events, 68.8 us)
Sparse Core Ops, SparseCore 0:
  80.3 17.4 all-gather.1

commit v4 on v3

v4 whole, which is shorter than its diff:
```python
import functools
import math

import jax
import jax.numpy as jnp
from jax import lax
from jax.experimental import pallas as pl
from jax.experimental.pallas import tpu as pltpu
from jax.sharding import PartitionSpec as P

epsilon = 1e-06
rope_base = 1000000.0
part_scale = 16.0


MESH = pl.DeviceIdType.MESH


def weight_kernel(
    n_head,
    w_key,
    w_value,
    w_query,
    fresh,
    q_gain,
    k_gain,
    cos_ref,
    sin_ref,
    out_ref,
    query_ref,
    new_key_ref,
    new_value_ref,
    wq,
    wk,
    wv,
    rows,
    q_acc,
    k_acc,
    v_acc,
    own_sem,
    load_sem,
    send_sem,
    z_sem,
    x_sem,
    c_sem,
    d_sem,
):
    group = lax.axis_index("group")
    store = lax.axis_index("store")
    head = lax.axis_index("head")
    part = w_key.shape[0] // n_head
    share = part // 4
    head_dim = w_key.shape[1]
    quarter = lax.rem(store, 4)
    x_quarter = lax.rem(quarter + 2, 4)
    x_mate = (group, store - quarter + x_quarter, head)
    c_mate = (group, store + 1 - 2 * lax.rem(store, 2), head)

    def head_peer(o):
        return (group, store, lax.rem(head + o, n_head))

    barrier = pltpu.get_barrier_semaphore()
    for peer in [head_peer(o) for o in range(1, n_head)] + [x_mate, c_mate]:
        pl.semaphore_signal(barrier, inc=1, device_id=peer, device_id_type=MESH)
    pl.semaphore_wait(barrier, n_head + 1)

    sends = []

    def send(src, dst, send_at, recv_at, peer):
        copy = pltpu.make_async_remote_copy(
            src_ref=src,
            dst_ref=dst,
            send_sem=send_at,
            recv_sem=recv_at,
            device_id=peer,
            device_id_type=MESH,
        )
        copy.start()
        sends.append(copy)
        return copy

    def share_rows(base, at):
        return pl.ds(pl.multiple_of(base + at * share, 16), share)

    first, second, third, fourth = {}, {}, {}, {}
    for o in range(1, n_head):
        target = lax.rem(head + o, n_head)
        for side, w in enumerate((w_key, w_value)):
            first[o, side] = send(
                w.at[share_rows(target * part, quarter)],
                out_ref.at[head, share_rows(0, quarter), side * head_dim : (side + 1) * head_dim],
                send_sem.at[side, o - 1],
                z_sem.at[side, o - 1],
                head_peer(o),
            )
    local = []
    for at, (src, dst) in enumerate(((fresh, rows), (w_query, wq), (w_key, wk), (w_value, wv))):
        local.append(pltpu.make_async_copy(src, dst, load_sem.at[at]))
    for side, w in enumerate((w_key, w_value)):
        local.append(
            pltpu.make_async_copy(
                w.at[pl.ds(pl.multiple_of(head * part, 16), part)],
                out_ref.at[head, :, side * head_dim : (side + 1) * head_dim],
                own_sem.at[side],
            )
        )
    for copy in local:
        copy.start()
    for copy in local[:4]:
        copy.wait()

    def project(o):
        cut = slice(o * part, (o + 1) * part)
        left = rows[:, cut]
        for acc, w in ((q_acc, wq), (k_acc, wk), (v_acc, wv)):
            term = jnp.dot(left, w[cut, :], preferred_element_type=jnp.float32)
            if o == 0:
                acc[...] = term
            else:
                acc[...] += term

    project(0)
    for o in range(1, n_head):
        source = lax.rem(head + n_head - o, n_head)
        first[o, 0].wait_recv()
        first[o, 1].wait_recv()
        slot = out_ref.at[source, share_rows(0, quarter)]
        second[o] = send(slot, slot, send_sem.at[2, o - 1], x_sem.at[o - 1], x_mate)
        third[o] = send(slot, slot, send_sem.at[3, o - 1], c_sem.at[o - 1], c_mate)
        project(o)
    for o in range(1, n_head):
        source = lax.rem(head + n_head - o, n_head)
        second[o].wait_recv()
        slot = out_ref.at[source, share_rows(0, x_quarter)]
        fourth[o] = send(slot, slot, send_sem.at[4, o - 1], d_sem.at[o - 1], c_mate)

    def turn(raw, gain):
        mean_sq = jnp.mean(raw * raw, axis=-1, keepdims=True)
        normed = raw * lax.rsqrt(mean_sq + epsilon) * gain
        turned = pltpu.roll(normed, head_dim // 2, 1)
        return (normed * cos_ref[...] + turned * sin_ref[...]).astype(jnp.bfloat16)

    for j in range(q_acc.shape[1] // head_dim):
        cut = slice(j * head_dim, (j + 1) * head_dim)
        query_ref[:, cut] = turn(q_acc[:, cut], q_gain[...])
    new_key_ref[...] = turn(k_acc[...], k_gain[...])
    new_value_ref[...] = v_acc[...].astype(jnp.bfloat16)

    for o in range(1, n_head):
        third[o].wait_recv()
        fourth[o].wait_recv()
    for copy in sends:
        copy.wait_send()
    for copy in local[4:]:
        copy.wait()


def gather_weights(n_head, w_key, w_value, w_query, rows, q_gain, k_gain, cosine, sine):
    features, head_dim = w_key.shape
    new_count = rows.shape[0]
    bf16, f32 = jnp.bfloat16, jnp.float32
    any_space = pl.BlockSpec(memory_space=pl.ANY)
    vmem = pl.BlockSpec(memory_space=pltpu.VMEM)
    dma = pltpu.SemaphoreType.DMA
    return pl.pallas_call(
        functools.partial(weight_kernel, n_head),
        out_shape=(
            jax.ShapeDtypeStruct((n_head, features // n_head, 2 * head_dim), bf16),
            jax.ShapeDtypeStruct((new_count, w_query.shape[1]), bf16),
            jax.ShapeDtypeStruct((new_count, head_dim), bf16),
            jax.ShapeDtypeStruct((new_count, head_dim), bf16),
        ),
        in_specs=[any_space] * 4 + [vmem] * 4,
        out_specs=[any_space] + [vmem] * 3,
        scratch_shapes=[
            pltpu.VMEM(w_query.shape, bf16),
            pltpu.VMEM(w_key.shape, bf16),
            pltpu.VMEM(w_value.shape, bf16),
            pltpu.VMEM(rows.shape, bf16),
            pltpu.VMEM((new_count, w_query.shape[1]), f32),
            pltpu.VMEM((new_count, head_dim), f32),
            pltpu.VMEM((new_count, head_dim), f32),
            dma((2,)),
            dma((4,)),
            dma((5, n_head - 1)),
            dma((2, n_head - 1)),
            dma((n_head - 1,)),
            dma((n_head - 1,)),
            dma((n_head - 1,)),
        ],
        compiler_params=pltpu.CompilerParams(
            collective_id=0, has_side_effects=True, vmem_limit_bytes=48 * 1024 * 1024
        ),
        cost_estimate=pl.CostEstimate(
            flops=2 * rows.size * 768, bytes_accessed=16 << 20, transcendentals=0
        ),
    )(w_key, w_value, w_query, rows, q_gain[None, :], k_gain[None, :], cosine, sine)


def page_kernel(
    scale, n_block, session_ref, q_ref, gain_ref, page_turn, row_turn, *refs
):
    pair_refs = refs[:n_block]
    numer_ref, denom_ref, numer, denom = refs[n_block:]
    page_len, head_dim = row_turn.shape[1:]
    numer[...] = jnp.zeros_like(numer)
    denom[...] = jnp.zeros_like(denom)
    gain = gain_ref[...]

    for block, pair_ref in enumerate(pair_refs):
        pages = pair_ref.shape[0] // page_len

        def body(i, carry):
            p = block * pages + i
            s = session_ref[p]
            here = pl.ds(pl.multiple_of(i * page_len, 8), page_len)
            raw = pair_ref[here, :head_dim]
            mean_sq = jnp.mean(raw * raw, axis=-1, keepdims=True)
            normed = raw * lax.rsqrt(mean_sq + epsilon) * gain
            turned = pltpu.roll(normed, head_dim // 2, 1)
            page_cos, page_sin = page_turn[p, 0:1, :], page_turn[p, 1:2, :]
            cosine = page_cos * row_turn[0] - page_sin * row_turn[1]
            sine = page_sin * row_turn[2] + page_cos * row_turn[3]
            keys = (normed * cosine + turned * sine).astype(jnp.bfloat16)
            values = pair_ref[here, head_dim:].astype(jnp.bfloat16)
            scores = jnp.dot(keys, q_ref[s], preferred_element_type=jnp.float32)
            weight = jnp.exp(scores * scale)
            denom[s] += jnp.sum(weight.reshape(page_len // 8, 8, weight.shape[-1]), axis=0)
            numer[s] += lax.dot_general(
                values,
                weight.astype(jnp.bfloat16),
                (((0,), (0,)), ((), ())),
                preferred_element_type=jnp.float32,
            )
            return carry

        lax.fori_loop(0, pages, body, 0, unroll=2)
    numer_ref[...] = numer[...].astype(jnp.bfloat16)
    denom_ref[...] = denom[...]


def page_attention(session_of, queries, gain, page_turn, row_turn, pairs, scale):
    sess_count, head_dim, columns = queries.shape
    return pl.pallas_call(
        functools.partial(page_kernel, scale, len(pairs)),
        out_shape=(
            jax.ShapeDtypeStruct((sess_count, head_dim, columns), jnp.bfloat16),
            jax.ShapeDtypeStruct((sess_count, 8, columns), jnp.float32),
        ),
        in_specs=[pl.BlockSpec(memory_space=pltpu.SMEM)]
        + [pl.BlockSpec(memory_space=pltpu.VMEM)] * (4 + len(pairs)),
        out_specs=[pl.BlockSpec(memory_space=pltpu.VMEM)] * 2,
        scratch_shapes=[
            pltpu.VMEM((sess_count, head_dim, columns), jnp.float32),
            pltpu.VMEM((sess_count, 8, columns), jnp.float32),
        ],
        compiler_params=pltpu.CompilerParams(vmem_limit_bytes=48 * 1024 * 1024),
        cost_estimate=pl.CostEstimate(
            flops=4 * pairs[0].size * len(pairs) * columns // 2, bytes_accessed=6 << 20, transcendentals=0
        ),
    )(session_of, queries, gain[None, :], page_turn, row_turn, *pairs)


def shards(saved, fresh, w_query, w_key, w_value, q_gain, k_gain, lengths, slot_page):
    page_count, page_len, part_width = saved.shape
    head_dim = w_key.shape[1]
    n_head = lax.axis_size("head")
    n_store = lax.axis_size("store")
    my_store = lax.axis_index("store")
    sess_count = lengths.shape[0]
    head = lax.axis_index("head")
    head = lax.axis_index("head")
    half = head_dim // 2
    freqs = jnp.exp(
        -jnp.arange(half, dtype=jnp.float32) * (2.0 / head_dim) * math.log(rope_base)
    )
    turn_rows = fresh[0]
    new_count = turn_rows.shape[0]
    group_heads = w_query.shape[1] // head_dim
    my_length = lax.dynamic_index_in_dim(lengths, my_store, 0, keepdims=False)
    new_pos = my_length * page_len + jnp.arange(new_count, dtype=jnp.int32)
    angles = new_pos.astype(jnp.float32)[:, None] * freqs[None, :]
    new_cos, new_sin = jnp.cos(angles), jnp.sin(angles)
    w_here, queries, new_keys, new_values = gather_weights(
        n_head,
        w_key,
        w_value,
        w_query,
        turn_rows,
        q_gain,
        k_gain,
        jnp.concatenate([new_cos, new_cos], axis=-1),
        jnp.concatenate([-new_sin, new_sin], axis=-1),
    )
    w_here, slot_page, lengths = lax.optimization_barrier((w_here, slot_page, lengths))

    n_block = 2 if page_count % 2 == 0 else 1
    block_pages = page_count // n_block
    products = [
        (
            jnp.einsum(
                "rf,hfc->hrc",
                saved[i * block_pages : (i + 1) * block_pages].reshape(-1, part_width),
                w_here,
                preferred_element_type=jnp.float32,
            )
            * part_scale
        ).astype(jnp.float16)
        for i in range(n_block)
    ]

    def product(block, target):
        return lax.dynamic_index_in_dim(block, target, 0, keepdims=False).astype(jnp.float32)

    ups = [None] * n_block
    downs = [None] * n_block
    for r in range(n_head - 1):
        up_to = jnp.minimum(n_head - 1 - r + head, n_head - 1)
        down_to = jnp.maximum(r - (n_head - 1) + head, 0)
        up_pairs = [(i, i + 1) for i in range(r + 1)]
        down_pairs = [(n_head - 1 - i, n_head - 2 - i) for i in range(r + 1)]
        for i, block in enumerate(products):
            up = product(block, up_to)
            down = product(block, down_to)
            if r > 0:
                up = up + ups[i].astype(jnp.float32)
                down = down + downs[i].astype(jnp.float32)
            ups[i] = lax.ppermute(up.astype(jnp.float16), "head", up_pairs)
            downs[i] = lax.ppermute(down.astype(jnp.float16), "head", down_pairs)
    pairs = []
    for i, block in enumerate(products):
        total = product(block, head) + (
            ups[i].astype(jnp.float32) + downs[i].astype(jnp.float32)
        )
        pairs.append(total * (1.0 / part_scale))

    ends = jnp.cumsum(lengths)
    starts = ends - lengths
    session_of = jnp.sum((slot_page[:, None] >= ends[None, :]).astype(jnp.int32), axis=1)
    onehot = (session_of[:, None] == jnp.arange(sess_count, dtype=jnp.int32)[None, :]).astype(
        jnp.int32
    )
    first_page = jnp.sum(onehot * starts[None, :], axis=1)
    page_pos = (slot_page - first_page) * page_len
    page_angle = page_pos.astype(jnp.float32)[:, None] * freqs[None, :]
    page_turn = jnp.stack([jnp.cos(page_angle), jnp.sin(page_angle)], axis=1)
    page_turn = jnp.concatenate([page_turn, page_turn], axis=-1)
    row_angle = jnp.arange(page_len, dtype=jnp.float32)[:, None] * freqs[None, :]
    cosine, sine = jnp.cos(row_angle), jnp.sin(row_angle)
    row_turn = jnp.stack(
        [
            jnp.concatenate([cosine, cosine], axis=-1),
            jnp.concatenate([sine, sine], axis=-1),
            jnp.concatenate([-cosine, cosine], axis=-1),
            jnp.concatenate([-sine, sine], axis=-1),
        ]
    )

    scale = 1.0 / math.sqrt(head_dim)
    columns = group_heads * new_count
    q_t = (
        queries.reshape(new_count, group_heads, head_dim)
        .transpose(2, 1, 0)
        .reshape(head_dim, columns)
    )
    every_query = lax.all_gather(q_t, "store", axis=0)

    numer_t, denom_8 = page_attention(
        session_of, every_query, k_gain, page_turn, row_turn, pairs, scale
    )
    denom = jnp.sum(denom_8, axis=1)
    high = denom.astype(jnp.bfloat16)
    low = (denom - high.astype(jnp.float32)).astype(jnp.bfloat16)
    sent = jnp.concatenate([numer_t, high[:, None, :], low[:, None, :]], axis=1)
    got = lax.all_to_all(sent, "store", 0, 0, tiled=True)
    total = jnp.sum(got.astype(jnp.float32), axis=0)

    own_scores = jnp.dot(new_keys, q_t, preferred_element_type=jnp.float32) * scale
    token = jnp.arange(columns, dtype=jnp.int32) % new_count
    causal = jnp.arange(new_count)[:, None] <= token[None, :]
    own_weight = jnp.where(causal, jnp.exp(own_scores), jnp.float32(0.0))
    own_denom = jnp.sum(own_weight, axis=0)
    own_numer = jnp.einsum(
        "kd,kc->dc", new_values, own_weight.astype(jnp.bfloat16), preferred_element_type=jnp.float32
    )
    numer = total[:head_dim] + own_numer
    denom = total[head_dim] + total[head_dim + 1] + own_denom
    attended = (numer / denom[None, :]).astype(jnp.bfloat16)
    attended = attended.reshape(head_dim, group_heads, new_count).transpose(2, 1, 0)
    return attended.reshape(1, new_count, group_heads * head_dim)


def solution(mesh):
    return jax.shard_map(
        shards,
        mesh=mesh,
        in_specs=(
            P(("group", "store"), None, "head"),
            P(("group", "store"), None, None),
            P(None, "head"),
            P(None, "head"),
            P(None, "head"),
            P(),
            P(),
            P("group"),
            P(("group", "store")),
        ),
        out_specs=P(("group", "store"), None, "head"),
        check_vma=False,
    )
```

time: 203 us -> 164 us (0.81); the launches traced: 200 us -> 163 us
  matrix products: 47.3 us -> 9.33 us
  waiting for transfers between devices: 20.8 us -> 37 us
  local copies, waits for them, and re-layouts: 28.8 us -> 15.8 us
    dot_general x16 -> x2, matrix products: 43.5 us -> 8.65 us  [shards(): jnp.einsum('rf,hfc->hrc', saved[i * block_pages:(i + 1) * block_pages].re...]
    ppermute x6, waiting for transfers between devices: 3.9 us -> 13.4 us  [shards(): downs[i] = lax.ppermute(down.astype(jnp.float16), 'head', down_pairs)]
    dot_general x1 -> x0, local copies, waits for them, and re-layouts: 7.84 us -> none  [shards(): jnp.dot(turn_rows, w_query, preferred_element_type=jnp.float32)]
    ppermute x6, waiting for transfers between devices: 3.36 us -> 8.94 us  [shards(): ups[i] = lax.ppermute(up.astype(jnp.float16), 'head', up_pairs)]
    convert_element_type x2 -> x4, other arithmetic: 0.98 us -> 6.53 us  [shards(): ups[i] = lax.ppermute(up.astype(jnp.float16), 'head', up_pairs)]
    neg x1, other arithmetic: 4.49 us -> 0.53 us  [shards(): -new_sin]
    concatenate x3 -> x2, other arithmetic: 4.09 us -> 0.25 us  [the longest x1 0.13 us: shards(): jnp.concatenate([new_cos, new_cos], axis=-1)]
    mul x2 -> x1, local copies, waits for them, and re-layouts: 3.68 us -> 0.07 us  [shards(): page_angle = page_pos.astype(jnp.float32)[:, None] * freqs[None, :]]
  transfers between devices with their start and end apart: 14 -> 14, of which waited for: 5 -> 6; matrix products, arithmetic and copies ran while one was open for 34% -> 14% of each run, Pallas kernels for 0% -> 0%
where the time goes in v4:
time: 164 us; the launch traced here: 163 us
  waiting for transfers between devices  37 us (23%)
  Pallas kernels  36.7 us (22%)
  starting transfers between devices  32.6 us (20%)
  other arithmetic  17.4 us (11%)
  local copies, waits for them, and re-layouts  15.8 us (10%)
  between operations  14.4 us (9%)
  matrix products  9.33 us (6%)
    pallas_call x1, Pallas kernels, gather_weights(): pl.pallas_call(functools.partial(weight_kernel, n_head), out_shape=(jax.S...  26.9 us
    ppermute x6, starting transfers between devices, shards(): ups[i] = lax.ppermute(up.astype(jnp.float16), 'head', up_pairs)  20.7 us
    all_to_all x1, waiting for transfers between devices, shards(): got = lax.all_to_all(sent, 'store', 0, 0, tiled=True)  14.7 us
    ppermute x6, waiting for transfers between devices, shards(): downs[i] = lax.ppermute(down.astype(jnp.float16), 'head', down_pairs)  13.4 us
    pallas_call x1, Pallas kernels, page_attention(): pl.pallas_call(functools.partial(page_kernel, scale, len(pairs)), out_sha...  9.81 us
    ppermute x6, waiting for transfers between devices, shards(): ups[i] = lax.ppermute(up.astype(jnp.float16), 'head', up_pairs)  8.94 us
    dot_general x2, matrix products, shards(): jnp.einsum('rf,hfc->hrc', saved[i * block_pages:(i + 1) * block_pages].re...  8.65 us
    ppermute x6, starting transfers between devices, shards(): downs[i] = lax.ppermute(down.astype(jnp.float16), 'head', down_pairs)  8.38 us
  transfers between devices with their start and end apart: 14, of which 6 were waited for; matrix products, arithmetic and copies ran while one was open for 14% of the time, Pallas kernels for 0%

profile of v4, /device:TPU:0, one launch (start us, length us, event | category | flops | bytes accessed | tf_op | source)
XLA Modules:
  0.0 163.4 jit_solution(659543972455530339)
XLA Ops:
  13.1 26.9 %shard_map.91 = (bf16[4,1280,256]{2,1,0:T(8,128)(2,1)S(1)}, bf16[256,512]{1,0:T(8,128)(2,1)S(1)}, bf16[256,128]{1,0:T(8,128)(2,1)S(1)}, bf16[256,128]{1,0:T(8,128)(2,1)S(1)}) custom-call(bf16[5120,128]{1,0:T(8,128)(2,1)S(1)} %copy-done, bf16[5120,128]{1,0:T(8,128)(2,1)S(1)} %copy-done.1, bf16[5120,512]{1,0:T(8,128)(2,1)} %w_query.1, ...), custom_call_target="tpu_custom_call" | custom-call | flops 2013265920 | bytes 16777216 | tf_op jit(solution)/shard_map/pallas_call | solution.py:165
  40.0 2.1 %fusion.24 = (bf16[12,64,1280]{2,1,0:T(8,128)(2,1)}, bf16[12,64,1280]{2,1,0:T(8,128)(2,1)}) fusion(bf16[24,64,1280]{2,1,0:T(8,128)(2,1)S(1)} %copy-done.9), kind=kLoop, calls=%fused_computation.71 | loop fusion | bytes 7864320 | tf_op jit(solution)/shard_map/slice | solution.py:303
  42.2 4.9 %multiply_convert_fusion = f16[4,256,768]{1,2,0:T(8,128)(2,1)} fusion(bf16[768,1280,1]{1,0,2:T(8,128)(2,1)} %bitcast.124, bf16[4,1280,256]{2,1,0:T(8,128)(2,1)S(1)} %get-tuple-element.18), kind=kOutput, calls=%fused_computation | convolution fusion | flops 2014838784 | bytes 6160384 | tf_op jit(solution)/shard_map/rf,hfc->hrc/dot_general | solution.py:301
  47.1 2.2 %dynamic-slice_bitcast_fusion.1 = (f16[768,256]{1,0:T(8,128)(2,1)}, f16[768,256]{1,0:T(8,128)(2,1)}) fusion(f16[4,256,768]{1,2,0:T(8,128)(2,1)} %multiply_convert_fusion, s32[]{:T(128)S(6)} %select_n.46, s32[]{:T(128)S(6)} %max.11), kind=kLoop, calls=%fused_computation.33 | loop fusion | bytes 1572872 | tf_op jit(solution)/shard_map/jit(dynamic_index_in_dim)/squeeze | solution.py:313
  49.3 3.3 %collective-permute-start.6 = (f16[768,256]{1,0:T(8,128)(2,1)}, f16[768,256]{1,0:T(8,128)(2,1)}, u32[]{:S(2)}, u32[]{:S(2)}) collective-permute-start(f16[768,256]{1,0:T(8,128)(2,1)} %get-tuple-element.27), channel_id=1, source_target_pairs={{0,1},{4,5},{8,9},{12,13},{16,17},{20,21},{24,25},{28,29}} | collective-permute-start | bytes 1179656 | tf_op jit(solution)/shard_map/ppermute | solution.py:328
  54.0 3.7 %multiply_convert_fusion.1 = f16[4,256,768]{1,2,0:T(8,128)(2,1)S(1)} fusion(bf16[768,1280,1]{1,0,2:T(8,128)(2,1)} %bitcast.123, bf16[4,1280,256]{2,1,0:T(8,128)(2,1)S(1)} %get-tuple-element.18), kind=kOutput, calls=%fused_computation.1 | convolution fusion | flops 2014838784 | bytes 6160384 | tf_op jit(solution)/shard_map/rf,hfc->hrc/dot_general | solution.py:301
  58.8 2.2 %collective-permute-start = (f16[768,256]{1,0:T(8,128)(2,1)}, f16[768,256]{1,0:T(8,128)(2,1)}, u32[]{:S(2)}, u32[]{:S(2)}) collective-permute-start(f16[768,256]{1,0:T(8,128)(2,1)} %get-tuple-element.31), channel_id=1, source_target_pairs={{0,1},{4,5},{8,9},{12,13},{16,17},{20,21},{24,25},{28,29}} | collective-permute-start | bytes 1179656 | tf_op jit(solution)/shard_map/ppermute | solution.py:328
  63.1 2.0 %copy.37 = bf16[1,128,1024]{2,1,0:T(8,128)(2,1)} copy(bf16[1,128,1024]{1,2,0:T(8,128)(2,1)} %bitcast.125) | data formatting | bytes 524288 | tf_op jit(solution)/shard_map/all_gather;reshape | solution.py:366
  68.1 1.9 %collective-permute-done = f16[768,256]{1,0:T(8,128)(2,1)} collective-permute-done((f16[768,256]{1,0:T(8,128)(2,1)}, f16[768,256]{1,0:T(8,128)(2,1)}, u32[]{:S(2)}, u32[]{:S(2)}) %collective-permute-start) | collective-permute-done | bytes 393248 | tf_op jit(solution)/shard_map/ppermute | solution.py:328
  71.1 4.4 %collective-permute-start.1 = (f16[768,256]{1,0:T(8,128)(2,1)S(1)}, f16[768,256]{1,0:T(8,128)(2,1)S(1)}, u32[]{:S(2)}, u32[]{:S(2)}) collective-permute-start(f16[768,256]{1,0:T(8,128)(2,1)S(1)} %fusion.11), channel_id=1, source_target_pairs={{0,1},{1,2},{4,5},{5,6},{8,9},{9,10},{12,13},{13,14},{16,17},{17,1... | collective-permute-start | bytes 1179656 | tf_op jit(solution)/shard_map/ppermute | solution.py:328
  75.5 2.8 %collective-permute-done.7 = f16[768,256]{1,0:T(8,128)(2,1)S(1)} collective-permute-done((f16[768,256]{1,0:T(8,128)(2,1)S(1)}, f16[768,256]{1,0:T(8,128)(2,1)S(1)}, u32[]{:S(2)}, u32[]{:S(2)}) %collective-permute-start.7) | collective-permute-done | bytes 393248 | tf_op jit(solution)/shard_map/ppermute | solution.py:328
  78.3 2.2 %fusion.7 = (f16[768,256]{1,0:T(8,128)(2,1)}, f16[768,256]{1,0:T(8,128)(2,1)}) fusion(f16[768,256]{1,0:T(8,128)(2,1)S(1)} %collective-permute-done.7, f16[4,256,768]{1,2,0:T(8,128)(2,1)S(1)} %copy-done.6, s32[]{:T(128)S(6)} %select_n.44, f16[768,256]{1,0:T(8,128)(2,1)} %collective-permute-done.9, s32[]{:T(128)S(6)} %max.10), kind=kLoop, calls=%fused_computation.18 | loop fusion | flops 1572864 | bytes 2359304 | tf_op jit(solution)/shard_map/convert_element_type | solution.py:328
  81.9 4.3 %collective-permute-done.1 = f16[768,256]{1,0:T(8,128)(2,1)S(1)} collective-permute-done((f16[768,256]{1,0:T(8,128)(2,1)S(1)}, f16[768,256]{1,0:T(8,128)(2,1)S(1)}, u32[]{:S(2)}, u32[]{:S(2)}) %collective-permute-start.1) | collective-permute-done | bytes 393248 | tf_op jit(solution)/shard_map/ppermute | solution.py:328
  86.2 2.1 %fusion.12 = (f16[768,256]{1,0:T(8,128)(2,1)}, f16[768,256]{1,0:T(8,128)(2,1)}) fusion(f16[768,256]{1,0:T(8,128)(2,1)S(1)} %collective-permute-done.1, f16[4,256,768]{1,2,0:T(8,128)(2,1)S(1)} %copy-done.8, s32[]{:T(128)S(6)} %select_n.44, f16[768,256]{1,0:T(8,128)(2,1)} %collective-permute-done.3, s32[]{:T(128)S(6)} %max.10), kind=kLoop, calls=%fused_computation.28 | loop fusion | flops 1572864 | bytes 2359304 | tf_op jit(solution)/shard_map/convert_element_type | solution.py:328
  90.8 5.0 %collective-permute-start.8 = (f16[768,256]{1,0:T(8,128)(2,1)}, f16[768,256]{1,0:T(8,128)(2,1)}, u32[]{:S(2)}, u32[]{:S(2)}) collective-permute-start(f16[768,256]{1,0:T(8,128)(2,1)} %get-tuple-element.25), channel_id=1, source_target_pairs={{0,1},{1,2},{2,3},{4,5},{5,6},{6,7},{8,9},{9,10},{10,11},{12,13},{... | collective-permute-start | bytes 1179656 | tf_op jit(solution)/shard_map/ppermute | solution.py:328
  95.9 4.6 %collective-permute-start.2 = (f16[768,256]{1,0:T(8,128)(2,1)}, f16[768,256]{1,0:T(8,128)(2,1)}, u32[]{:S(2)}, u32[]{:S(2)}) collective-permute-start(f16[768,256]{1,0:T(8,128)(2,1)} %get-tuple-element.29), channel_id=1, source_target_pairs={{0,1},{1,2},{2,3},{4,5},{5,6},{6,7},{8,9},{9,10},{10,11},{12,13},{... | collective-permute-start | bytes 1179656 | tf_op jit(solution)/shard_map/ppermute | solution.py:328
  100.4 1.9 %fusion.5 = f16[768,256]{1,0:T(8,128)(2,1)} fusion(f16[768,256]{1,0:T(8,128)(2,1)} %collective-permute-done.10, f16[4,256,768]{1,2,0:T(8,128)(2,1)S(1)} %copy-done.6, s32[]{:T(128)S(6)} %max.9), kind=kLoop, calls=%fused_computation.14 | loop fusion | flops 786432 | bytes 1179652 | tf_op jit(solution)/shard_map/convert_element_type | solution.py:329
  103.6 1.9 %fusion.10 = f16[768,256]{1,0:T(8,128)(2,1)} fusion(f16[768,256]{1,0:T(8,128)(2,1)} %collective-permute-done.4, f16[4,256,768]{1,2,0:T(8,128)(2,1)S(1)} %copy-done.8, s32[]{:T(128)S(6)} %max.9), kind=kLoop, calls=%fused_computation.24 | loop fusion | flops 786432 | bytes 1179652 | tf_op jit(solution)/shard_map/convert_element_type | solution.py:329
  105.5 1.5 collective-permute-start.5
  107.9 8.5 %collective-permute-done.11 = f16[768,256]{1,0:T(8,128)(2,1)S(1)} collective-permute-done((f16[768,256]{1,0:T(8,128)(2,1)}, f16[768,256]{1,0:T(8,128)(2,1)S(1)}, u32[]{:S(2)}, u32[]{:S(2)}) %collective-permute-start.11) | collective-permute-done | bytes 393248 | tf_op jit(solution)/shard_map/ppermute | solution.py:329
  117.7 4.8 %collective-permute-done.5 = f16[768,256]{1,0:T(8,128)(2,1)S(1)} collective-permute-done((f16[768,256]{1,0:T(8,128)(2,1)}, f16[768,256]{1,0:T(8,128)(2,1)S(1)}, u32[]{:S(2)}, u32[]{:S(2)}) %collective-permute-start.5) | collective-permute-done | bytes 393248 | tf_op jit(solution)/shard_map/ppermute | solution.py:329
  125.1 9.8 %shard_map.92 = (bf16[4,128,1024]{2,1,0:T(8,128)(2,1)S(1)}, f32[4,8,1024]{2,1,0:T(8,128)S(1)}) custom-call(s32[24]{0:T(128)S(1)} %convert_reduce_fusion.1.session_ref, bf16[4,128,1024]{2,1,0:T(8,128)(2,1)S(1)} %copy-done.5, f32[1,128]{1,0:T(1,128)S(1)} %bitcast.121, f32[24,2,128]{2,1,0:T(2,128)S(1)} %maximum_maximum_fusion.page_turn, ...), custom_call_target="tpu_custom_call" | custom-call | flops 805306368 | bytes 6291456 | tf_op jit(solution)/shard_map/pallas_call | solution.py:244
  136.2 3.5 %all-to-all-start = ((bf16[4,130,1024]{2,1,0:T(8,128)(2,1)}), bf16[4,130,1024]{2,1,0:T(8,128)(2,1)S(1)}, u32[]{:S(2)}, u32[]{:S(2)}) async-start(bf16[4,130,1024]{2,1,0:T(8,128)(2,1)} %pad_maximum_fusion), calls=%async_computation | async-start | bytes 2228224 | tf_op jit(solution)/shard_map/all_to_all | solution.py:375
  140.2 14.7 %all-to-all-done = bf16[4,130,1024]{2,1,0:T(8,128)(2,1)S(1)} async-done(((bf16[4,130,1024]{2,1,0:T(8,128)(2,1)}), bf16[4,130,1024]{2,1,0:T(8,128)(2,1)S(1)}, u32[]{:S(2)}, u32[]{:S(2)}) %all-to-all-start) | async-done | bytes 1064992 | tf_op jit(solution)/shard_map/all_to_all | solution.py:375
  (76 shorter events, 27.9 us)
Async XLA Ops:
  6.5 117.3 %all-gather.2.cloned.1.call-start = ((), (), s32[]{:S(2)}) async-start(), calls=%async_computation.1 | async-start | bytes 1310720 | tf_op jit(solution)/shard_map/all_gather | solution.py:366
  9.1 1.3 copy-start
  10.5 1.3 copy-start.1
  13.1 26.9 %copy-start.9 = (bf16[24,64,1280]{2,1,0:T(8,128)(2,1)S(1)}, bf16[24,64,1280]{2,1,0:T(8,128)(2,1)}, u32[]{:S(2)}) copy-start(bf16[24,64,1280]{2,1,0:T(8,128)(2,1)} %param.9) | copy-start | bytes 11796484
  49.3 16.3 %collective-permute-start.6 = (f16[768,256]{1,0:T(8,128)(2,1)}, f16[768,256]{1,0:T(8,128)(2,1)}, u32[]{:S(2)}, u32[]{:S(2)}) collective-permute-start(f16[768,256]{1,0:T(8,128)(2,1)} %get-tuple-element.27), channel_id=1, source_target_pairs={{0,1},{4,5},{8,9},{12,13},{16,17},{20,21},{24,25},{28,29}} | collective-permute-start | bytes 1179656 | tf_op jit(solution)/shard_map/ppermute | solution.py:328
  52.5 23.0 %collective-permute-start.9 = (f16[768,256]{1,0:T(8,128)(2,1)}, f16[768,256]{1,0:T(8,128)(2,1)}, u32[]{:S(2)}, u32[]{:S(2)}) collective-permute-start(f16[768,256]{1,0:T(8,128)(2,1)} %get-tuple-element.28), channel_id=1, source_target_pairs={{3,2},{7,6},{11,10},{15,14},{19,18},{23,22},{27,26},{31,30}} | collective-permute-start | bytes 1179656 | tf_op jit(solution)/shard_map/ppermute | solution.py:329
  57.7 5.4 %copy-start.7 = (f16[4,256,768]{1,2,0:T(8,128)(2,1)}, f16[4,256,768]{1,2,0:T(8,128)(2,1)S(1)}, u32[]{:S(2)}) copy-start(f16[4,256,768]{1,2,0:T(8,128)(2,1)S(1)} %multiply_convert_fusion.1) | copy-start | bytes 4718596
  57.7 7.5 %copy-start.11 = (s32[4]{0:T(128)S(1)}, s32[4]{0:T(128)}, u32[]{:S(2)}) copy-start(s32[4]{0:T(128)} %param.16) | copy-start | bytes 52
  57.7 7.7 %copy-start.12 = (s32[24]{0:T(128)S(1)}, s32[24]{0:T(128)}, u32[]{:S(2)}) copy-start(s32[24]{0:T(128)} %param.17) | copy-start | bytes 292
  57.7 7.9 %copy-start.6 = (f16[4,256,768]{1,2,0:T(8,128)(2,1)S(1)}, f16[4,256,768]{1,2,0:T(8,128)(2,1)}, u32[]{:S(2)}) copy-start(f16[4,256,768]{1,2,0:T(8,128)(2,1)} %multiply_convert_fusion) | copy-start | bytes 4718596
  58.8 11.2 %collective-permute-start = (f16[768,256]{1,0:T(8,128)(2,1)}, f16[768,256]{1,0:T(8,128)(2,1)}, u32[]{:S(2)}, u32[]{:S(2)}) collective-permute-start(f16[768,256]{1,0:T(8,128)(2,1)} %get-tuple-element.31), channel_id=1, source_target_pairs={{0,1},{4,5},{8,9},{12,13},{16,17},{20,21},{24,25},{28,29}} | collective-permute-start | bytes 1179656 | tf_op jit(solution)/shard_map/ppermute | solution.py:328
  61.0 20.9 %collective-permute-start.3 = (f16[768,256]{1,0:T(8,128)(2,1)}, f16[768,256]{1,0:T(8,128)(2,1)}, u32[]{:S(2)}, u32[]{:S(2)}) collective-permute-start(f16[768,256]{1,0:T(8,128)(2,1)} %get-tuple-element.32), channel_id=1, source_target_pairs={{3,2},{7,6},{11,10},{15,14},{19,18},{23,22},{27,26},{31,30}} | collective-permute-start | bytes 1179656 | tf_op jit(solution)/shard_map/ppermute | solution.py:329
  63.1 6.9 %copy-start.8 = (f16[4,256,768]{1,2,0:T(8,128)(2,1)S(1)}, f16[4,256,768]{1,2,0:T(8,128)(2,1)}, u32[]{:S(2)}) copy-start(f16[4,256,768]{1,2,0:T(8,128)(2,1)} %copy-done.7) | copy-start | bytes 4718596
  66.8 11.5 %collective-permute-start.7 = (f16[768,256]{1,0:T(8,128)(2,1)S(1)}, f16[768,256]{1,0:T(8,128)(2,1)S(1)}, u32[]{:S(2)}, u32[]{:S(2)}) collective-permute-start(f16[768,256]{1,0:T(8,128)(2,1)S(1)} %fusion.6), channel_id=1, source_target_pairs={{0,1},{1,2},{4,5},{5,6},{8,9},{9,10},{12,13},{13,14},{16,17},{17,1... | collective-permute-start | bytes 1179656 | tf_op jit(solution)/shard_map/ppermute | solution.py:328
  71.1 15.1 %collective-permute-start.1 = (f16[768,256]{1,0:T(8,128)(2,1)S(1)}, f16[768,256]{1,0:T(8,128)(2,1)S(1)}, u32[]{:S(2)}, u32[]{:S(2)}) collective-permute-start(f16[768,256]{1,0:T(8,128)(2,1)S(1)} %fusion.11), channel_id=1, source_target_pairs={{0,1},{1,2},{4,5},{5,6},{8,9},{9,10},{12,13},{13,14},{16,17},{17,1... | collective-permute-start | bytes 1179656 | tf_op jit(solution)/shard_map/ppermute | solution.py:328
  80.5 20.0 %collective-permute-start.10 = (f16[768,256]{1,0:T(8,128)(2,1)}, f16[768,256]{1,0:T(8,128)(2,1)}, u32[]{:S(2)}, u32[]{:S(2)}) collective-permute-start(f16[768,256]{1,0:T(8,128)(2,1)} %get-tuple-element.26), channel_id=1, source_target_pairs={{3,2},{2,1},{7,6},{6,5},{11,10},{10,9},{15,14},{14,13},{19,18},{18... | collective-permute-start | bytes 1179656 | tf_op jit(solution)/shard_map/ppermute | solution.py:329
  88.3 15.3 %collective-permute-start.4 = (f16[768,256]{1,0:T(8,128)(2,1)}, f16[768,256]{1,0:T(8,128)(2,1)}, u32[]{:S(2)}, u32[]{:S(2)}) collective-permute-start(f16[768,256]{1,0:T(8,128)(2,1)} %get-tuple-element.30), channel_id=1, source_target_pairs={{3,2},{2,1},{7,6},{6,5},{11,10},{10,9},{15,14},{14,13},{19,18},{18... | collective-permute-start | bytes 1179656 | tf_op jit(solution)/shard_map/ppermute | solution.py:329
  90.8 17.1 %collective-permute-start.8 = (f16[768,256]{1,0:T(8,128)(2,1)}, f16[768,256]{1,0:T(8,128)(2,1)}, u32[]{:S(2)}, u32[]{:S(2)}) collective-permute-start(f16[768,256]{1,0:T(8,128)(2,1)} %get-tuple-element.25), channel_id=1, source_target_pairs={{0,1},{1,2},{2,3},{4,5},{5,6},{6,7},{8,9},{9,10},{10,11},{12,13},{... | collective-permute-start | bytes 1179656 | tf_op jit(solution)/shard_map/ppermute | solution.py:328
  95.9 21.8 %collective-permute-start.2 = (f16[768,256]{1,0:T(8,128)(2,1)}, f16[768,256]{1,0:T(8,128)(2,1)}, u32[]{:S(2)}, u32[]{:S(2)}) collective-permute-start(f16[768,256]{1,0:T(8,128)(2,1)} %get-tuple-element.29), channel_id=1, source_target_pairs={{0,1},{1,2},{2,3},{4,5},{5,6},{6,7},{8,9},{9,10},{10,11},{12,13},{... | collective-permute-start | bytes 1179656 | tf_op jit(solution)/shard_map/ppermute | solution.py:328
  102.3 14.1 %collective-permute-start.11 = (f16[768,256]{1,0:T(8,128)(2,1)}, f16[768,256]{1,0:T(8,128)(2,1)S(1)}, u32[]{:S(2)}, u32[]{:S(2)}) collective-permute-start(f16[768,256]{1,0:T(8,128)(2,1)} %fusion.5), channel_id=1, source_target_pairs={{3,2},{2,1},{1,0},{7,6},{6,5},{5,4},{11,10},{10,9},{9,8},{15,14},{... | collective-permute-start | bytes 1179656 | tf_op jit(solution)/shard_map/ppermute | solution.py:329
  105.5 17.1 %collective-permute-start.5 = (f16[768,256]{1,0:T(8,128)(2,1)}, f16[768,256]{1,0:T(8,128)(2,1)S(1)}, u32[]{:S(2)}, u32[]{:S(2)}) collective-permute-start(f16[768,256]{1,0:T(8,128)(2,1)} %fusion.10), channel_id=1, source_target_pairs={{3,2},{2,1},{1,0},{7,6},{6,5},{5,4},{11,10},{10,9},{9,8},{15,14},{... | collective-permute-start | bytes 1179656 | tf_op jit(solution)/shard_map/ppermute | solution.py:329
  107.9 16.0 %copy-start.4 = (f32[128]{0:T(128)S(1)}, f32[128]{0:T(128)}, u32[]{:S(2)}) copy-start(f32[128]{0:T(128)} %param.15) | copy-start | bytes 1540
  135.0 4.7 %copy-start.10 = (bf16[256,4,128]{2,0,1:T(8,128)(2,1)S(1)}, bf16[256,4,128]{2,0,1:T(8,128)(2,1)}, u32[]{:S(2)}) copy-start(bf16[256,4,128]{2,0,1:T(8,128)(2,1)} %copy_bitcast_fusion) | copy-start | bytes 786436
  136.2 18.7 %all-to-all-start = ((bf16[4,130,1024]{2,1,0:T(8,128)(2,1)}), bf16[4,130,1024]{2,1,0:T(8,128)(2,1)S(1)}, u32[]{:S(2)}, u32[]{:S(2)}) async-start(bf16[4,130,1024]{2,1,0:T(8,128)(2,1)} %pad_maximum_fusion), calls=%async_computation | async-start | bytes 2228224 | tf_op jit(solution)/shard_map/all_to_all | solution.py:375
  (3 other events, 2.5 us)
Sparse Core Ops, SparseCore 0:
  65.2 17.4 all-gather.1

commit v5 on v4

--- a/solution.py
+++ b/solution.py
@@ -294,7 +294,7 @@
     )
     w_here, slot_page, lengths = lax.optimization_barrier((w_here, slot_page, lengths))
 
-    n_block = 2 if page_count % 2 == 0 else 1
+    n_block = 3 if page_count % 3 == 0 else 1
     block_pages = page_count // n_block
     products = [
         (
@@ -369,10 +369,35 @@
         session_of, every_query, k_gain, page_turn, row_turn, pairs, scale
     )
     denom = jnp.sum(denom_8, axis=1)
-    high = denom.astype(jnp.bfloat16)
-    low = (denom - high.astype(jnp.float32)).astype(jnp.bfloat16)
-    sent = jnp.concatenate([numer_t, high[:, None, :], low[:, None, :]], axis=1)
-    got = lax.all_to_all(sent, "store", 0, 0, tiled=True)
+
+    def packed(numer, denom):
+        high = denom.astype(jnp.bfloat16)
+        low = (denom - high.astype(jnp.float32)).astype(jnp.bfloat16)
+        return jnp.concatenate(
+            [numer.astype(jnp.bfloat16), high[:, None, :], low[:, None, :]], axis=1
+        )
+
+    core = lax.rem(my_store, 2)
+
+    def of_core(array, c):
+        cut = array.reshape((n_store // 2, 2) + array.shape[1:])
+        return lax.dynamic_index_in_dim(cut, c, 1, keepdims=False)
+
+    came = lax.ppermute(
+        packed(of_core(numer_t, 1 - core), of_core(denom, 1 - core)),
+        "store",
+        [(i, i + 1 - 2 * (i % 2)) for i in range(n_store)],
+    ).astype(jnp.float32)
+    chip_numer = of_core(numer_t, core).astype(jnp.float32) + came[:, :head_dim]
+    chip_denom = of_core(denom, core) + came[:, head_dim] + came[:, head_dim + 1]
+    got = lax.all_to_all(
+        packed(chip_numer, chip_denom),
+        "store",
+        0,
+        0,
+        tiled=True,
+        axis_index_groups=[list(range(c, n_store, 2)) for c in range(2)],
+    )
     total = jnp.sum(got.astype(jnp.float32), axis=0)
 
     own_scores = jnp.dot(new_keys, q_t, preferred_element_type=jnp.float32) * scale

time: 164 us -> 153 us (0.933)
  waiting for transfers between devices: 37 us -> 25.7 us
  starting transfers between devices: 32.6 us -> 41.5 us
  other arithmetic: 17.4 us -> 10.4 us
    ppermute x6 -> x9, waiting for transfers between devices: 8.94 us -> 0.02 us  [shards(): ups[i] = lax.ppermute(up.astype(jnp.float16), 'head', up_pairs)]
    ppermute x6 -> x9, starting transfers between devices: 20.7 us -> 28.5 us  [shards(): ups[i] = lax.ppermute(up.astype(jnp.float16), 'head', up_pairs)]
    all_to_all x1, waiting for transfers between devices: 14.7 us -> 8.45 us  [shards(): lax.all_to_all(packed(chip_numer, chip_denom), 'store', 0, 0, tiled=True,...]
    convert_element_type x2 -> x3, other arithmetic: 3.74 us -> 0.32 us  [shards(): downs[i] = lax.ppermute(down.astype(jnp.float16), 'head', down_pairs)]
    mul x2 -> x3, other arithmetic: 2.54 us -> 0.35 us  [shards(): pairs.append(total * (1.0 / part_scale))]
    ppermute x6 -> x9, waiting for transfers between devices: 13.4 us -> 15.3 us  [shards(): downs[i] = lax.ppermute(down.astype(jnp.float16), 'head', down_pairs)]
    ppermute x0 -> x1, waiting for transfers between devices: none -> 1.9 us  [shards(): lax.ppermute(packed(of_core(numer_t, 1 - core), of_core(denom, 1 - core))...]
    ppermute x6 -> x9, starting transfers between devices: 8.38 us -> 9.48 us  [shards(): downs[i] = lax.ppermute(down.astype(jnp.float16), 'head', down_pairs)]
  transfers between devices with their start and end apart: 14 -> 21, of which waited for: 6 -> 5; matrix products, arithmetic and copies ran while one was open for 14% -> 10% of each run, Pallas kernels for 0% -> 0%
where the time goes in v5:
time: 153 us; the launch traced here: 152 us
  starting transfers between devices  41.5 us (27%)
  Pallas kernels  36.7 us (24%)
  waiting for transfers between devices  25.7 us (17%)
  between operations  14.7 us (10%)
  local copies, waits for them, and re-layouts  14.3 us (9%)
  other arithmetic  10.4 us (7%)
  matrix products  8.96 us (6%)
    ppermute x9, starting transfers between devices, shards(): ups[i] = lax.ppermute(up.astype(jnp.float16), 'head', up_pairs)  28.5 us
    pallas_call x1, Pallas kernels, gather_weights(): pl.pallas_call(functools.partial(weight_kernel, n_head), out_shape=(jax.S...  26.9 us
    ppermute x9, waiting for transfers between devices, shards(): downs[i] = lax.ppermute(down.astype(jnp.float16), 'head', down_pairs)  15.3 us
    pallas_call x1, Pallas kernels, page_attention(): pl.pallas_call(functools.partial(page_kernel, scale, len(pairs)), out_sha...  9.79 us
    ppermute x9, starting transfers between devices, shards(): downs[i] = lax.ppermute(down.astype(jnp.float16), 'head', down_pairs)  9.48 us
    all_to_all x1, waiting for transfers between devices, shards(): lax.all_to_all(packed(chip_numer, chip_denom), 'store', 0, 0, tiled=True,...  8.45 us
    dot_general x3, matrix products, shards(): jnp.einsum('rf,hfc->hrc', saved[i * block_pages:(i + 1) * block_pages].re...  8.28 us
    convert_element_type x6, other arithmetic, shards(): ups[i] = lax.ppermute(up.astype(jnp.float16), 'head', up_pairs)  5.77 us
  transfers between devices with their start and end apart: 21, of which 5 were waited for; matrix products, arithmetic and copies ran while one was open for 10% of the time, Pallas kernels for 0%

profile of v5, /device:TPU:0, one launch (start us, length us, event | category | flops | bytes accessed | tf_op | source)
XLA Modules:
  0.0 152.3 jit_solution(5582947866929241813)
XLA Ops:
  13.1 26.9 %shard_map.91 = (bf16[4,1280,256]{2,1,0:T(8,128)(2,1)S(1)}, bf16[256,512]{1,0:T(8,128)(2,1)S(1)}, bf16[256,128]{1,0:T(8,128)(2,1)S(1)}, bf16[256,128]{1,0:T(8,128)(2,1)S(1)}) custom-call(bf16[5120,128]{1,0:T(8,128)(2,1)S(1)} %copy-done, bf16[5120,128]{1,0:T(8,128)(2,1)S(1)} %copy-done.1, bf16[5120,512]{1,0:T(8,128)(2,1)} %w_query.1, ...), custom_call_target="tpu_custom_call" | custom-call | flops 2013265920 | bytes 16777216 | tf_op jit(solution)/shard_map/pallas_call | solution.py:165
  40.0 2.0 %fusion.32 = (bf16[8,64,1280]{2,1,0:T(8,128)(2,1)}, bf16[8,64,1280]{2,1,0:T(8,128)(2,1)}, bf16[8,64,1280]{2,1,0:T(8,128)(2,1)}) fusion(bf16[24,64,1280]{2,1,0:T(8,128)(2,1)S(1)} %copy-done.6), kind=kLoop, calls=%fused_computation.95 | loop fusion | bytes 7864320 | tf_op jit(solution)/shard_map/slice | solution.py:303
  42.0 3.8 %multiply_convert_fusion = f16[4,256,512]{1,2,0:T(8,128)(2,1)} fusion(bf16[512,1280,1]{1,0,2:T(8,128)(2,1)} %bitcast.180, bf16[4,1280,256]{2,1,0:T(8,128)(2,1)S(1)} %get-tuple-element.18), kind=kOutput, calls=%fused_computation | convolution fusion | flops 1343225856 | bytes 4980736 | tf_op jit(solution)/shard_map/rf,hfc->hrc/dot_general | solution.py:301
  45.8 1.9 %dynamic-slice_bitcast_fusion.1 = (f16[512,256]{1,0:T(8,128)(2,1)}, f16[512,256]{1,0:T(8,128)(2,1)}) fusion(f16[4,256,512]{1,2,0:T(8,128)(2,1)} %multiply_convert_fusion, s32[]{:T(128)S(6)} %select_n.63, s32[]{:T(128)S(6)} %max.11), kind=kLoop, calls=%fused_computation.50 | loop fusion | bytes 1048584 | tf_op jit(solution)/shard_map/jit(dynamic_index_in_dim)/squeeze | solution.py:313
  47.7 3.2 %collective-permute-start.12 = (f16[512,256]{1,0:T(8,128)(2,1)}, f16[512,256]{1,0:T(8,128)(2,1)}, u32[]{:S(2)}, u32[]{:S(2)}) collective-permute-start(f16[512,256]{1,0:T(8,128)(2,1)} %get-tuple-element.30), channel_id=1, source_target_pairs={{0,1},{4,5},{8,9},{12,13},{16,17},{20,21},{24,25},{28,29}} | collective-permute-start | bytes 786440 | tf_op jit(solution)/shard_map/ppermute | solution.py:328
  52.3 2.9 %multiply_convert_fusion.1 = f16[4,256,512]{1,2,0:T(8,128)(2,1)S(1)} fusion(bf16[512,1280,1]{1,0,2:T(8,128)(2,1)} %bitcast.179, bf16[4,1280,256]{2,1,0:T(8,128)(2,1)S(1)} %get-tuple-element.18), kind=kOutput, calls=%fused_computation.1 | convolution fusion | flops 1343225856 | bytes 4980736 | tf_op jit(solution)/shard_map/rf,hfc->hrc/dot_general | solution.py:301
  56.3 2.0 %collective-permute-start.6 = (f16[512,256]{1,0:T(8,128)(2,1)}, f16[512,256]{1,0:T(8,128)(2,1)}, u32[]{:S(2)}, u32[]{:S(2)}) collective-permute-start(f16[512,256]{1,0:T(8,128)(2,1)} %get-tuple-element.34), channel_id=1, source_target_pairs={{0,1},{4,5},{8,9},{12,13},{16,17},{20,21},{24,25},{28,29}} | collective-permute-start | bytes 786440 | tf_op jit(solution)/shard_map/ppermute | solution.py:328
  58.3 1.4 collective-permute-start.9
  59.6 1.5 %multiply_convert_fusion.2 = f16[4,256,512]{1,2,0:T(8,128)(2,1)S(1)} fusion(bf16[512,1280,1]{1,0,2:T(8,128)(2,1)S(1)} %bitcast.178, bf16[4,1280,256]{2,1,0:T(8,128)(2,1)S(1)} %get-tuple-element.18), kind=kOutput, calls=%fused_computation.2 | convolution fusion | flops 1343225856 | bytes 4980736 | tf_op jit(solution)/shard_map/rf,hfc->hrc/dot_general | solution.py:301
  61.3 2.1 %collective-permute-start = (f16[512,256]{1,0:T(8,128)(2,1)S(1)}, f16[512,256]{1,0:T(8,128)(2,1)}, u32[]{:S(2)}, u32[]{:S(2)}) collective-permute-start(f16[512,256]{1,0:T(8,128)(2,1)S(1)} %get-tuple-element.38), channel_id=1, source_target_pairs={{0,1},{4,5},{8,9},{12,13},{16,17},{20,21},{24,25},{28,29}} | collective-permute-start | bytes 786440 | tf_op jit(solution)/shard_map/ppermute | solution.py:328
  67.4 1.4 collective-permute-start.13
  70.0 4.2 %collective-permute-start.7 = (f16[512,256]{1,0:T(8,128)(2,1)S(1)}, f16[512,256]{1,0:T(8,128)(2,1)S(1)}, u32[]{:S(2)}, u32[]{:S(2)}) collective-permute-start(f16[512,256]{1,0:T(8,128)(2,1)S(1)} %fusion.12), channel_id=1, source_target_pairs={{0,1},{1,2},{4,5},{5,6},{8,9},{9,10},{12,13},{13,14},{16,17},{17,1... | collective-permute-start | bytes 786440 | tf_op jit(solution)/shard_map/ppermute | solution.py:328
  75.3 2.1 %collective-permute-start.1 = (f16[512,256]{1,0:T(8,128)(2,1)S(1)}, f16[512,256]{1,0:T(8,128)(2,1)S(1)}, u32[]{:S(2)}, u32[]{:S(2)}) collective-permute-start(f16[512,256]{1,0:T(8,128)(2,1)S(1)} %fusion.17), channel_id=1, source_target_pairs={{0,1},{1,2},{4,5},{5,6},{8,9},{9,10},{12,13},{13,14},{16,17},{17,1... | collective-permute-start | bytes 786440 | tf_op jit(solution)/shard_map/ppermute | solution.py:328
  79.2 3.2 %collective-permute-start.14 = (f16[512,256]{1,0:T(8,128)(2,1)S(1)}, f16[512,256]{1,0:T(8,128)(2,1)S(1)}, u32[]{:S(2)}, u32[]{:S(2)}) collective-permute-start(f16[512,256]{1,0:T(8,128)(2,1)S(1)} %get-tuple-element.28), channel_id=1, source_target_pairs={{0,1},{1,2},{2,3},{4,5},{5,6},{6,7},{8,9},{9,10},{10,11},{12,13},{... | collective-permute-start | bytes 786440 | tf_op jit(solution)/shard_map/ppermute | solution.py:328
  84.3 5.2 %collective-permute-start.8 = (f16[512,256]{1,0:T(8,128)(2,1)S(1)}, f16[512,256]{1,0:T(8,128)(2,1)S(1)}, u32[]{:S(2)}, u32[]{:S(2)}) collective-permute-start(f16[512,256]{1,0:T(8,128)(2,1)S(1)} %get-tuple-element.32), channel_id=1, source_target_pairs={{0,1},{1,2},{2,3},{4,5},{5,6},{6,7},{8,9},{9,10},{10,11},{12,13},{... | collective-permute-start | bytes 786440 | tf_op jit(solution)/shard_map/ppermute | solution.py:328
  90.4 5.2 %collective-permute-start.2 = (f16[512,256]{1,0:T(8,128)(2,1)S(1)}, f16[512,256]{1,0:T(8,128)(2,1)S(1)}, u32[]{:S(2)}, u32[]{:S(2)}) collective-permute-start(f16[512,256]{1,0:T(8,128)(2,1)S(1)} %get-tuple-element.36), channel_id=1, source_target_pairs={{0,1},{1,2},{2,3},{4,5},{5,6},{6,7},{8,9},{9,10},{10,11},{12,13},{... | collective-permute-start | bytes 786440 | tf_op jit(solution)/shard_map/ppermute | solution.py:328
  98.5 1.5 collective-permute-start.5
  100.0 7.4 %collective-permute-done.17 = f16[512,256]{1,0:T(8,128)(2,1)S(1)} collective-permute-done((f16[512,256]{1,0:T(8,128)(2,1)S(1)}, f16[512,256]{1,0:T(8,128)(2,1)S(1)}, u32[]{:S(2)}, u32[]{:S(2)}) %collective-permute-start.17) | collective-permute-done | bytes 262176 | tf_op jit(solution)/shard_map/ppermute | solution.py:329
  107.5 5.2 %collective-permute-done.11 = f16[512,256]{1,0:T(8,128)(2,1)S(1)} collective-permute-done((f16[512,256]{1,0:T(8,128)(2,1)S(1)}, f16[512,256]{1,0:T(8,128)(2,1)S(1)}, u32[]{:S(2)}, u32[]{:S(2)}) %collective-permute-start.11) | collective-permute-done | bytes 262176 | tf_op jit(solution)/shard_map/ppermute | solution.py:329
  112.9 2.7 %collective-permute-done.5 = f16[512,256]{1,0:T(8,128)(2,1)S(1)} collective-permute-done((f16[512,256]{1,0:T(8,128)(2,1)S(1)}, f16[512,256]{1,0:T(8,128)(2,1)S(1)}, u32[]{:S(2)}, u32[]{:S(2)}) %collective-permute-start.5) | collective-permute-done | bytes 262176 | tf_op jit(solution)/shard_map/ppermute | solution.py:329
  116.9 9.8 %shard_map.92 = (bf16[4,128,1024]{2,1,0:T(8,128)(2,1)S(1)}, f32[4,8,1024]{2,1,0:T(8,128)S(1)}) custom-call(s32[24]{0:T(128)S(1)} %convert_reduce_fusion.1.session_ref, bf16[4,128,1024]{2,1,0:T(8,128)(2,1)S(1)} %copy-done.5, f32[1,128]{1,0:T(1,128)S(1)} %bitcast.175, f32[24,2,128]{2,1,0:T(2,128)S(1)} %maximum_maximum_fusion.page_turn, ...), custom_call_target="tpu_custom_call" | custom-call | flops 805306368 | bytes 6291456 | tf_op jit(solution)/shard_map/pallas_call | solution.py:244
  128.3 1.9 %collective-permute-done.18 = bf16[2,130,1024]{2,0,1:T(2,128)(2,1)S(1)} collective-permute-done((bf16[2,130,1024]{2,0,1:T(2,128)(2,1)S(1)}, bf16[2,130,1024]{2,0,1:T(2,128)(2,1)S(1)}, u32[]{:S(2)}, u32[]{:S(2)}) %collective-permute-start.18) | collective-permute-done | bytes 532512 | tf_op jit(solution)/shard_map/ppermute | solution.py:386
  131.5 3.5 %all-to-all-start = ((bf16[2,130,1024]{2,1,0:T(8,128)(2,1)}), bf16[2,130,1024]{2,1,0:T(8,128)(2,1)S(1)}, u32[]{:S(2)}, u32[]{:S(2)}) async-start(bf16[2,130,1024]{2,1,0:T(8,128)(2,1)} %pad_maximum_fusion), calls=%async_computation | async-start | bytes 1114112 | tf_op jit(solution)/shard_map/all_to_all | solution.py:393
  135.4 8.5 %all-to-all-done = bf16[2,130,1024]{2,1,0:T(8,128)(2,1)S(1)} async-done(((bf16[2,130,1024]{2,1,0:T(8,128)(2,1)}), bf16[2,130,1024]{2,1,0:T(8,128)(2,1)S(1)}, u32[]{:S(2)}, u32[]{:S(2)}) %all-to-all-start) | async-done | bytes 532512 | tf_op jit(solution)/shard_map/all_to_all | solution.py:393
  (110 shorter events, 28.3 us)
Async XLA Ops:
  6.5 109.1 %all-gather.2.cloned.1.call-start = ((), (), s32[]{:S(2)}) async-start(), calls=%async_computation.1 | async-start | bytes 1310720 | tf_op jit(solution)/shard_map/all_gather | solution.py:366
  13.1 26.9 %copy-start.6 = (bf16[24,64,1280]{2,1,0:T(8,128)(2,1)S(1)}, bf16[24,64,1280]{2,1,0:T(8,128)(2,1)}, u32[]{:S(2)}) copy-start(bf16[24,64,1280]{2,1,0:T(8,128)(2,1)} %param.9) | copy-start | bytes 11796484
  47.7 17.9 %collective-permute-start.12 = (f16[512,256]{1,0:T(8,128)(2,1)}, f16[512,256]{1,0:T(8,128)(2,1)}, u32[]{:S(2)}, u32[]{:S(2)}) collective-permute-start(f16[512,256]{1,0:T(8,128)(2,1)} %get-tuple-element.30), channel_id=1, source_target_pairs={{0,1},{4,5},{8,9},{12,13},{16,17},{20,21},{24,25},{28,29}} | collective-permute-start | bytes 786440 | tf_op jit(solution)/shard_map/ppermute | solution.py:328
  50.9 24.4 %collective-permute-start.15 = (f16[512,256]{1,0:T(8,128)(2,1)}, f16[512,256]{1,0:T(8,128)(2,1)}, u32[]{:S(2)}, u32[]{:S(2)}) collective-permute-start(f16[512,256]{1,0:T(8,128)(2,1)} %get-tuple-element.31), channel_id=1, source_target_pairs={{3,2},{7,6},{11,10},{15,14},{19,18},{23,22},{27,26},{31,30}} | collective-permute-start | bytes 786440 | tf_op jit(solution)/shard_map/ppermute | solution.py:329
  56.3 11.2 %collective-permute-start.6 = (f16[512,256]{1,0:T(8,128)(2,1)}, f16[512,256]{1,0:T(8,128)(2,1)}, u32[]{:S(2)}, u32[]{:S(2)}) collective-permute-start(f16[512,256]{1,0:T(8,128)(2,1)} %get-tuple-element.34), channel_id=1, source_target_pairs={{0,1},{4,5},{8,9},{12,13},{16,17},{20,21},{24,25},{28,29}} | collective-permute-start | bytes 786440 | tf_op jit(solution)/shard_map/ppermute | solution.py:328
  58.3 21.0 %collective-permute-start.9 = (f16[512,256]{1,0:T(8,128)(2,1)}, f16[512,256]{1,0:T(8,128)(2,1)}, u32[]{:S(2)}, u32[]{:S(2)}) collective-permute-start(f16[512,256]{1,0:T(8,128)(2,1)} %get-tuple-element.35), channel_id=1, source_target_pairs={{3,2},{7,6},{11,10},{15,14},{19,18},{23,22},{27,26},{31,30}} | collective-permute-start | bytes 786440 | tf_op jit(solution)/shard_map/ppermute | solution.py:329
  61.3 8.6 %collective-permute-start = (f16[512,256]{1,0:T(8,128)(2,1)S(1)}, f16[512,256]{1,0:T(8,128)(2,1)}, u32[]{:S(2)}, u32[]{:S(2)}) collective-permute-start(f16[512,256]{1,0:T(8,128)(2,1)S(1)} %get-tuple-element.38), channel_id=1, source_target_pairs={{0,1},{4,5},{8,9},{12,13},{16,17},{20,21},{24,25},{28,29}} | collective-permute-start | bytes 786440 | tf_op jit(solution)/shard_map/ppermute | solution.py:328
  65.7 18.6 %collective-permute-start.3 = (f16[512,256]{1,0:T(8,128)(2,1)S(1)}, f16[512,256]{1,0:T(8,128)(2,1)S(1)}, u32[]{:S(2)}, u32[]{:S(2)}) collective-permute-start(f16[512,256]{1,0:T(8,128)(2,1)S(1)} %get-tuple-element.39), channel_id=1, source_target_pairs={{3,2},{7,6},{11,10},{15,14},{19,18},{23,22},{27,26},{31,30}} | collective-permute-start | bytes 786440 | tf_op jit(solution)/shard_map/ppermute | solution.py:329
  67.4 9.9 %collective-permute-start.13 = (f16[512,256]{1,0:T(8,128)(2,1)S(1)}, f16[512,256]{1,0:T(8,128)(2,1)S(1)}, u32[]{:S(2)}, u32[]{:S(2)}) collective-permute-start(f16[512,256]{1,0:T(8,128)(2,1)S(1)} %fusion.7), channel_id=1, source_target_pairs={{0,1},{1,2},{4,5},{5,6},{8,9},{9,10},{12,13},{13,14},{16,17},{17,1... | collective-permute-start | bytes 786440 | tf_op jit(solution)/shard_map/ppermute | solution.py:328
  70.0 12.4 %collective-permute-start.7 = (f16[512,256]{1,0:T(8,128)(2,1)S(1)}, f16[512,256]{1,0:T(8,128)(2,1)S(1)}, u32[]{:S(2)}, u32[]{:S(2)}) collective-permute-start(f16[512,256]{1,0:T(8,128)(2,1)S(1)} %fusion.12), channel_id=1, source_target_pairs={{0,1},{1,2},{4,5},{5,6},{8,9},{9,10},{12,13},{13,14},{16,17},{17,1... | collective-permute-start | bytes 786440 | tf_op jit(solution)/shard_map/ppermute | solution.py:328
  75.3 14.2 %copy-start.11 = (f16[4,256,512]{1,2,0:T(8,128)(2,1)S(1)}, f16[4,256,512]{1,2,0:T(8,128)(2,1)}, u32[]{:S(2)}) copy-start(f16[4,256,512]{1,2,0:T(8,128)(2,1)} %copy-done.10) | copy-start | bytes 3145732
  75.3 14.2 %collective-permute-start.1 = (f16[512,256]{1,0:T(8,128)(2,1)S(1)}, f16[512,256]{1,0:T(8,128)(2,1)S(1)}, u32[]{:S(2)}, u32[]{:S(2)}) collective-permute-start(f16[512,256]{1,0:T(8,128)(2,1)S(1)} %fusion.17), channel_id=1, source_target_pairs={{0,1},{1,2},{4,5},{5,6},{8,9},{9,10},{12,13},{13,14},{16,17},{17,1... | collective-permute-start | bytes 786440 | tf_op jit(solution)/shard_map/ppermute | solution.py:328
  78.5 11.8 %collective-permute-start.16 = (f16[512,256]{1,0:T(8,128)(2,1)S(1)}, f16[512,256]{1,0:T(8,128)(2,1)S(1)}, u32[]{:S(2)}, u32[]{:S(2)}) collective-permute-start(f16[512,256]{1,0:T(8,128)(2,1)S(1)} %get-tuple-element.29), channel_id=1, source_target_pairs={{3,2},{2,1},{7,6},{6,5},{11,10},{10,9},{15,14},{14,13},{19,18},{18... | collective-permute-start | bytes 786440 | tf_op jit(solution)/shard_map/ppermute | solution.py:329
  79.2 19.2 %collective-permute-start.14 = (f16[512,256]{1,0:T(8,128)(2,1)S(1)}, f16[512,256]{1,0:T(8,128)(2,1)S(1)}, u32[]{:S(2)}, u32[]{:S(2)}) collective-permute-start(f16[512,256]{1,0:T(8,128)(2,1)S(1)} %get-tuple-element.28), channel_id=1, source_target_pairs={{0,1},{1,2},{2,3},{4,5},{5,6},{6,7},{8,9},{9,10},{10,11},{12,13},{... | collective-permute-start | bytes 786440 | tf_op jit(solution)/shard_map/ppermute | solution.py:328
  83.6 12.0 %collective-permute-start.10 = (f16[512,256]{1,0:T(8,128)(2,1)S(1)}, f16[512,256]{1,0:T(8,128)(2,1)S(1)}, u32[]{:S(2)}, u32[]{:S(2)}) collective-permute-start(f16[512,256]{1,0:T(8,128)(2,1)S(1)} %get-tuple-element.33), channel_id=1, source_target_pairs={{3,2},{2,1},{7,6},{6,5},{11,10},{10,9},{15,14},{14,13},{19,18},{18... | collective-permute-start | bytes 786440 | tf_op jit(solution)/shard_map/ppermute | solution.py:329
  84.3 23.2 %collective-permute-start.8 = (f16[512,256]{1,0:T(8,128)(2,1)S(1)}, f16[512,256]{1,0:T(8,128)(2,1)S(1)}, u32[]{:S(2)}, u32[]{:S(2)}) collective-permute-start(f16[512,256]{1,0:T(8,128)(2,1)S(1)} %get-tuple-element.32), channel_id=1, source_target_pairs={{0,1},{1,2},{2,3},{4,5},{5,6},{6,7},{8,9},{9,10},{10,11},{12,13},{... | collective-permute-start | bytes 786440 | tf_op jit(solution)/shard_map/ppermute | solution.py:328
  89.7 7.4 %collective-permute-start.4 = (f16[512,256]{1,0:T(8,128)(2,1)S(1)}, f16[512,256]{1,0:T(8,128)(2,1)S(1)}, u32[]{:S(2)}, u32[]{:S(2)}) collective-permute-start(f16[512,256]{1,0:T(8,128)(2,1)S(1)} %get-tuple-element.37), channel_id=1, source_target_pairs={{3,2},{2,1},{7,6},{6,5},{11,10},{10,9},{15,14},{14,13},{19,18},{18... | collective-permute-start | bytes 786440 | tf_op jit(solution)/shard_map/ppermute | solution.py:329
  90.4 22.5 %collective-permute-start.2 = (f16[512,256]{1,0:T(8,128)(2,1)S(1)}, f16[512,256]{1,0:T(8,128)(2,1)S(1)}, u32[]{:S(2)}, u32[]{:S(2)}) collective-permute-start(f16[512,256]{1,0:T(8,128)(2,1)S(1)} %get-tuple-element.36), channel_id=1, source_target_pairs={{0,1},{1,2},{2,3},{4,5},{5,6},{6,7},{8,9},{9,10},{10,11},{12,13},{... | collective-permute-start | bytes 786440 | tf_op jit(solution)/shard_map/ppermute | solution.py:328
  95.6 11.8 %collective-permute-start.17 = (f16[512,256]{1,0:T(8,128)(2,1)S(1)}, f16[512,256]{1,0:T(8,128)(2,1)S(1)}, u32[]{:S(2)}, u32[]{:S(2)}) collective-permute-start(f16[512,256]{1,0:T(8,128)(2,1)S(1)} %fusion.6), channel_id=1, source_target_pairs={{3,2},{2,1},{1,0},{7,6},{6,5},{5,4},{11,10},{10,9},{9,8},{15,14},{... | collective-permute-start | bytes 786440 | tf_op jit(solution)/shard_map/ppermute | solution.py:329
  97.1 15.7 %collective-permute-start.11 = (f16[512,256]{1,0:T(8,128)(2,1)S(1)}, f16[512,256]{1,0:T(8,128)(2,1)S(1)}, u32[]{:S(2)}, u32[]{:S(2)}) collective-permute-start(f16[512,256]{1,0:T(8,128)(2,1)S(1)} %fusion.11), channel_id=1, source_target_pairs={{3,2},{2,1},{1,0},{7,6},{6,5},{5,4},{11,10},{10,9},{9,8},{15,14},{... | collective-permute-start | bytes 786440 | tf_op jit(solution)/shard_map/ppermute | solution.py:329
  98.5 17.1 %collective-permute-start.5 = (f16[512,256]{1,0:T(8,128)(2,1)S(1)}, f16[512,256]{1,0:T(8,128)(2,1)S(1)}, u32[]{:S(2)}, u32[]{:S(2)}) collective-permute-start(f16[512,256]{1,0:T(8,128)(2,1)S(1)} %fusion.16), channel_id=1, source_target_pairs={{3,2},{2,1},{1,0},{7,6},{6,5},{5,4},{11,10},{10,9},{9,8},{15,14},{... | collective-permute-start | bytes 786440 | tf_op jit(solution)/shard_map/ppermute | solution.py:329
  107.5 8.2 %copy-start.4 = (f32[128]{0:T(128)S(1)}, f32[128]{0:T(128)}, u32[]{:S(2)}) copy-start(f32[128]{0:T(128)} %param.15) | copy-start | bytes 1540
  128.3 2.0 %collective-permute-start.18 = (bf16[2,130,1024]{2,0,1:T(2,128)(2,1)S(1)}, bf16[2,130,1024]{2,0,1:T(2,128)(2,1)S(1)}, u32[]{:S(2)}, u32[]{:S(2)}) collective-permute-start(bf16[2,130,1024]{2,0,1:T(2,128)(2,1)S(1)} %pad_maximum_fusion.1), channel_id=1, source_target_pairs={{0,4},{4,0},{8,12},{12,8},{1,5},{5,1},{9,13},{13,9},{2,6},{6,2},{1... | collective-permute-start | bytes 1597448 | tf_op jit(solution)/shard_map/ppermute | solution.py:386
  131.5 12.4 %all-to-all-start = ((bf16[2,130,1024]{2,1,0:T(8,128)(2,1)}), bf16[2,130,1024]{2,1,0:T(8,128)(2,1)S(1)}, u32[]{:S(2)}, u32[]{:S(2)}) async-start(bf16[2,130,1024]{2,1,0:T(8,128)(2,1)} %pad_maximum_fusion), calls=%async_computation | async-start | bytes 1114112 | tf_op jit(solution)/shard_map/all_to_all | solution.py:393
  (12 other events, 38.2 us)
Sparse Core Ops, SparseCore 0:
  64.5 16.8 all-gather.1
